TPU v7x, 128 devices: a whole 4x4x4 slice. The times are simulated.
128 devices in a mesh: dp: 16 (over y, z_lo, core), tensor: 8 (over z_hi, x).
Axes of the slice: x: 4, y: 4, z: 4 (z_hi: 2, z_lo: 2; z = z_hi * 2 + z_lo), core: 2. Of those that a mesh axis runs over, the one named last changes fastest.
Arguments:
- layer_input: bfloat16 [16384, 1024], P(('dp', 'tensor')), may hold values from -6 to 6
- cotangent: bfloat16 [16384, 1024], P(('dp', 'tensor')), may hold values from -6 to 6
- segment: int32 [16384], P('dp'), may hold values from 0 to 2, as said below
- live_mask: int32 [16384], P('dp'), may hold values from 0 to 1, as said below
- query_weight: bfloat16 [2, 1024, 1024], P(None, 'dp', 'tensor'), may hold values from -0.1875 to 0.1875
- key_weight: bfloat16 [2, 1024, 1024], P(None, 'dp', 'tensor'), may hold values from -0.1875 to 0.1875
- value_weight: bfloat16 [2, 1024, 1024], P(None, 'dp', 'tensor'), may hold values from -0.1875 to 0.1875
- out_weight: bfloat16 [2, 1024, 1024], P(None, 'tensor', 'dp'), may hold values from -3 to 3
- up_weight: bfloat16 [2, 1024, 4096], P(None, 'dp', 'tensor'), may hold values from -0.1875 to 0.1875
- down_weight: bfloat16 [2, 4096, 1024], P(None, 'tensor', 'dp'), may hold values from -0.09375 to 0.09375
- query_bias: float32 [2, 1024], P(None, 'tensor'), may hold values from -3 to 3
- value_bias: float32 [2, 1024], P(None, 'tensor'), may hold values from -3 to 3
- up_bias: float32 [2, 4096], P(None, 'tensor'), may hold values from -3 to 3
- out_bias: float32 [2, 1024], replicated, may hold values from -3 to 3
- down_bias: float32 [2, 1024], replicated, may hold values from -3 to 3
- attention_gain: float32 [2, 1024], replicated, may hold values from 0.5 to 1.5
- attention_shift: float32 [2, 1024], replicated, may hold values from -3 to 3
- output_gain: float32 [2, 1024], replicated, may hold values from 0.5 to 1.5
- output_shift: float32 [2, 1024], replicated, may hold values from -3 to 3
Outputs:
- layer_output: float32 [16384, 1024], P(('dp', 'tensor'))
- input_grad: float32 [16384, 1024], P(('dp', 'tensor'))
- query_weight_grad: float32 [2, 1024, 1024], P(None, 'dp', 'tensor')
- key_weight_grad: float32 [2, 1024, 1024], P(None, 'dp', 'tensor')
- value_weight_grad: float32 [2, 1024, 1024], P(None, 'dp', 'tensor')
- out_weight_grad: float32 [2, 1024, 1024], P(None, 'tensor', 'dp')
- up_weight_grad: float32 [2, 1024, 4096], P(None, 'dp', 'tensor')
- down_weight_grad: float32 [2, 4096, 1024], P(None, 'tensor', 'dp')
- query_bias_grad: float32 [2, 1024], P(None, 'tensor')
- value_bias_grad: float32 [2, 1024], P(None, 'tensor')
- up_bias_grad: float32 [2, 4096], P(None, 'tensor')
- out_bias_grad: float32 [2, 1024], replicated
- down_bias_grad: float32 [2, 1024], replicated
- attention_gain_grad: float32 [2, 1024], replicated
- attention_shift_grad: float32 [2, 1024], replicated
- output_gain_grad: float32 [2, 1024], replicated
- output_shift_grad: float32 [2, 1024], replicated
Inputs may be any that keep to these rules, and one draw needn't show every extreme that they name: Within each aligned block of 1024 positions the segment numbers are 0, 1, 2 in that order, never falling, each present. `live_mask`: within each segment the ones form a prefix of one or more positions.
All inputs are finite; a program needn't handle non-finite values.
Results may differ from a plain program's by a relative error of at most 0.039.
Values may be sent and summed in bfloat16 or wider, within the bound.
No kernel may reach another device: no remote copies, remote signals or barrier semaphores. Data moves between devices by JAX's collectives and lax.ppermute only.
A program may use at most 128 MiB of HBM per device.

v0:
```python
import math

import jax
import jax.numpy as jnp
from jax import lax
from jax.sharding import PartitionSpec as P

HEAD_DIM = 64


NORM_EPS = 1e-12
MASKED = -1000000000.0


def normalize(rows, gain, shift):
    center = rows - jnp.mean(rows, axis=-1, keepdims=True)
    spread = jnp.mean(center * center, axis=-1, keepdims=True)
    return center * lax.rsqrt(spread + NORM_EPS) * gain + shift


def gelu_exact(values):
    return jax.nn.gelu(values, approximate=False)


def product(left, right):
    return jnp.dot(left, right, preferred_element_type=jnp.float32)


def inner_left(left, right):
    return lax.dot_general(
        left, right, (((0,), (0,)), ((), ())), preferred_element_type=jnp.float32
    )


def inner_right(left, right):
    return lax.dot_general(
        left, right, (((1,), (1,)), ((), ())), preferred_element_type=jnp.float32
    )


def block_layout(queries):
    group_len, local_width = queries.shape
    head_count = local_width // HEAD_DIM
    block_rows = math.gcd(group_len, 512)
    return (group_len, local_width, head_count, block_rows, group_len // block_rows)


def attend(queries, key_rows, value_rows, segment, live_mask):
    group_len, local_width, head_count, block_rows, block_count = block_layout(queries)
    score_scale = HEAD_DIM ** (-0.5)
    key_heads = key_rows.reshape(group_len, head_count, HEAD_DIM)
    value_heads = value_rows.reshape(group_len, head_count, HEAD_DIM)
    query_blocks = queries.reshape(block_count, block_rows, head_count, HEAD_DIM)
    seg_blocks = segment.reshape(block_count, block_rows)

    def one_block(pieces):
        query_part, seg_part = pieces
        scores = (
            jnp.einsum("qhd,khd->hqk", query_part, key_heads, preferred_element_type=jnp.float32)
            * score_scale
        )
        allowed = (seg_part[:, None] == segment[None, :]) & (live_mask[None, :] == 1)
        scores = jnp.where(allowed[None], scores, MASKED)
        row_max = jnp.max(scores, axis=-1, keepdims=True)
        exp_scores = jnp.exp(scores - row_max)
        row_total = jnp.sum(exp_scores, axis=-1, keepdims=True)
        soft = (exp_scores / row_total).astype(jnp.bfloat16)
        mixed = jnp.einsum("hqk,khd->qhd", soft, value_heads, preferred_element_type=jnp.float32)
        return (mixed.astype(jnp.bfloat16), (row_max + jnp.log(row_total))[..., 0])

    mixed, log_totals = lax.map(one_block, (query_blocks, seg_blocks))
    return (mixed.reshape(group_len, local_width), log_totals)


def attend_back(queries, key_rows, value_rows, segment, live_mask, log_totals, grad_mixed):
    group_len, local_width, head_count, block_rows, block_count = block_layout(queries)
    score_scale = HEAD_DIM ** (-0.5)
    key_heads = key_rows.reshape(group_len, head_count, HEAD_DIM)
    value_heads = value_rows.reshape(group_len, head_count, HEAD_DIM)
    query_blocks = queries.reshape(block_count, block_rows, head_count, HEAD_DIM)
    seg_blocks = segment.reshape(block_count, block_rows)
    grad_blocks = grad_mixed.reshape(block_count, block_rows, head_count, HEAD_DIM)

    def one_block(running, pieces):
        key_acc, value_acc = running
        query_part, seg_part, total_part, grad_part = pieces
        scores = (
            jnp.einsum("qhd,khd->hqk", query_part, key_heads, preferred_element_type=jnp.float32)
            * score_scale
        )
        allowed = (seg_part[:, None] == segment[None, :]) & (live_mask[None, :] == 1)
        scores = jnp.where(allowed[None], scores, MASKED)
        soft = jnp.exp(scores - total_part[..., None])
        soft_low = soft.astype(jnp.bfloat16)
        grad_soft = jnp.einsum(
            "qhd,khd->hqk", grad_part, value_heads, preferred_element_type=jnp.float32
        ).astype(jnp.bfloat16)
        row_dot = jnp.sum(grad_soft * soft, axis=-1, keepdims=True)
        grad_scores = (soft * (grad_soft - row_dot)).astype(jnp.bfloat16)
        grad_query = (
            jnp.einsum("hqk,khd->qhd", grad_scores, key_heads, preferred_element_type=jnp.float32)
            * score_scale
        )
        key_acc = (
            key_acc
            + jnp.einsum(
                "hqk,qhd->khd", grad_scores, query_part, preferred_element_type=jnp.float32
            )
            * score_scale
        )
        value_acc = value_acc + jnp.einsum(
            "hqk,qhd->khd", soft_low, grad_part, preferred_element_type=jnp.float32
        )
        return ((key_acc, value_acc), grad_query.astype(jnp.bfloat16))

    zeros = jnp.zeros((group_len, head_count, HEAD_DIM), jnp.float32)
    (key_acc, value_acc), grad_query = lax.scan(
        one_block, (zeros, zeros), (query_blocks, seg_blocks, log_totals, grad_blocks)
    )
    return (
        grad_query.reshape(group_len, local_width),
        key_acc.reshape(group_len, local_width).astype(jnp.bfloat16),
        value_acc.reshape(group_len, local_width).astype(jnp.bfloat16),
    )


def on_device(
    layer_input,
    cotangent,
    segment,
    live_mask,
    query_weight,
    key_weight,
    value_weight,
    out_weight,
    up_weight,
    down_weight,
    query_bias,
    value_bias,
    up_bias,
    out_bias,
    down_bias,
    attention_gain,
    attention_shift,
    output_gain,
    output_shift,
):
    layers = query_weight.shape[0]

    def gather_rows(rows):
        return lax.all_gather(rows, "tensor", axis=0, tiled=True)

    def sum_heads(partial_value):
        return lax.psum_scatter(partial_value, "tensor", scatter_dimension=0, tiled=True)

    def gather_grads(rows):
        return lax.all_gather(rows, "tensor", axis=0, tiled=True)

    def sum_grads(partial_value):
        return lax.psum_scatter(partial_value, "tensor", scatter_dimension=0, tiled=True)

    current = layer_input.astype(jnp.float32)
    saved = []
    fetched = []
    for layer in range(layers):
        mats = (
            lax.all_gather(query_weight[layer], "dp", axis=0, tiled=True),
            lax.all_gather(key_weight[layer], "dp", axis=0, tiled=True),
            lax.all_gather(value_weight[layer], "dp", axis=0, tiled=True),
            lax.all_gather(out_weight[layer], "dp", axis=1, tiled=True),
            lax.all_gather(up_weight[layer], "dp", axis=0, tiled=True),
            lax.all_gather(down_weight[layer], "dp", axis=1, tiled=True),
        )
        (
            forward_query_mat,
            forward_key_mat,
            forward_value_mat,
            forward_out_mat,
            forward_up_mat,
            forward_down_mat,
        ) = mats
        forward_gathered_in = gather_rows(current.astype(jnp.bfloat16))
        forward_queries = (
            product(forward_gathered_in, forward_query_mat) + query_bias[layer]
        ).astype(jnp.bfloat16)
        forward_key_rows = product(forward_gathered_in, forward_key_mat).astype(jnp.bfloat16)
        forward_value_rows = (
            product(forward_gathered_in, forward_value_mat) + value_bias[layer]
        ).astype(jnp.bfloat16)
        forward_attended, forward_log_totals = attend(
            forward_queries, forward_key_rows, forward_value_rows, segment, live_mask
        )
        forward_first_sum = (
            current + sum_heads(product(forward_attended, forward_out_mat)) + out_bias[layer]
        )
        normed_mid = normalize(forward_first_sum, attention_gain[layer], attention_shift[layer])
        forward_gathered_mid = gather_rows(normed_mid.astype(jnp.bfloat16))
        forward_pre_gelu = product(forward_gathered_mid, forward_up_mat) + up_bias[layer]
        forward_activated = gelu_exact(forward_pre_gelu).astype(jnp.bfloat16)
        forward_second_sum = (
            normed_mid + sum_heads(product(forward_activated, forward_down_mat)) + down_bias[layer]
        )
        normed_out = normalize(forward_second_sum, output_gain[layer], output_shift[layer])
        forward_kept = (
            forward_gathered_in,
            forward_queries,
            forward_key_rows,
            forward_value_rows,
            forward_attended,
            forward_log_totals,
            forward_first_sum,
            forward_gathered_mid,
            forward_pre_gelu,
            forward_activated,
            forward_second_sum,
        )
        current = normed_out
        saved.append(forward_kept)
        fetched.append(mats)
    grad_rows = cotangent.astype(jnp.float32)
    mat_grads = [None] * layers
    small_grads = [None] * layers
    for layer in reversed(range(layers)):
        mats = (
            lax.all_gather(query_weight[layer], "dp", axis=0, tiled=True),
            lax.all_gather(key_weight[layer], "dp", axis=0, tiled=True),
            lax.all_gather(value_weight[layer], "dp", axis=0, tiled=True),
            lax.all_gather(out_weight[layer], "dp", axis=1, tiled=True),
            lax.all_gather(up_weight[layer], "dp", axis=0, tiled=True),
            lax.all_gather(down_weight[layer], "dp", axis=1, tiled=True),
        )
        backward_kept = saved[layer]
        (
            gathered_in,
            queries,
            key_rows,
            value_rows,
            attended,
            log_totals,
            first_sum,
            gathered_mid,
            pre_gelu,
            activated,
            second_sum,
        ) = backward_kept
        query_mat, key_mat, value_mat, out_mat, up_mat, down_mat = mats
        unused, second_back = jax.vjp(
            normalize, second_sum, output_gain[layer], output_shift[layer]
        )
        grad_second, grad_out_gain, grad_out_shift = second_back(grad_rows)
        grad_branch = grad_second.astype(jnp.bfloat16)
        down_bias_term = jnp.sum(grad_branch, axis=0, dtype=jnp.float32)
        branch_all = gather_grads(grad_branch)
        down_grad = inner_left(activated, branch_all)
        grad_activated = inner_right(branch_all, down_mat)
        unused, gelu_back = jax.vjp(gelu_exact, pre_gelu)
        grad_pre = gelu_back(grad_activated)[0].astype(jnp.bfloat16)
        up_bias_term = jnp.sum(grad_pre, axis=0, dtype=jnp.float32)
        up_grad = inner_left(gathered_mid, grad_pre)
        grad_mid = grad_second + sum_grads(inner_right(grad_pre, up_mat))
        unused, first_back = jax.vjp(
            normalize, first_sum, attention_gain[layer], attention_shift[layer]
        )
        grad_first, grad_att_gain, grad_att_shift = first_back(grad_mid)
        grad_attn = grad_first.astype(jnp.bfloat16)
        out_bias_term = jnp.sum(grad_attn, axis=0, dtype=jnp.float32)
        attn_all = gather_grads(grad_attn)
        out_grad = inner_left(attended, attn_all)
        grad_attended = inner_right(attn_all, out_mat).astype(jnp.bfloat16)
        grad_queries, grad_keys, grad_values = attend_back(
            queries, key_rows, value_rows, segment, live_mask, log_totals, grad_attended
        )
        query_bias_term = jnp.sum(grad_queries, axis=0, dtype=jnp.float32)
        value_bias_term = jnp.sum(grad_values, axis=0, dtype=jnp.float32)
        query_grad = inner_left(gathered_in, grad_queries)
        key_grad = inner_left(gathered_in, grad_keys)
        value_grad = inner_left(gathered_in, grad_values)
        back_in = (
            inner_right(grad_queries, query_mat)
            + inner_right(grad_keys, key_mat)
            + inner_right(grad_values, value_mat)
        )
        grad_in = grad_first + sum_grads(back_in)
        mat_terms = (query_grad, key_grad, value_grad, out_grad, up_grad, down_grad)
        small_terms = (
            query_bias_term,
            value_bias_term,
            up_bias_term,
            out_bias_term,
            down_bias_term,
            grad_att_gain,
            grad_att_shift,
            grad_out_gain,
            grad_out_shift,
        )
        grad_rows, mat_terms, small_terms = (grad_in, mat_terms, small_terms)
        mat_grads[layer] = (
            lax.psum_scatter(mat_terms[0], "dp", scatter_dimension=0, tiled=True),
            lax.psum_scatter(mat_terms[1], "dp", scatter_dimension=0, tiled=True),
            lax.psum_scatter(mat_terms[2], "dp", scatter_dimension=0, tiled=True),
            lax.psum_scatter(mat_terms[3], "dp", scatter_dimension=1, tiled=True),
            lax.psum_scatter(mat_terms[4], "dp", scatter_dimension=0, tiled=True),
            lax.psum_scatter(mat_terms[5], "dp", scatter_dimension=1, tiled=True),
        )
        small_grads[layer] = small_terms
    stacked = [
        jnp.stack([mat_grads[layer][index] for layer in range(layers)]) for index in range(6)
    ]
    small_stacked = [
        jnp.stack([small_grads[layer][index] for layer in range(layers)]) for index in range(9)
    ]
    head_sums = lax.psum((small_stacked[0], small_stacked[1], small_stacked[2]), "dp")
    row_sums = lax.psum(
        (
            small_stacked[3],
            small_stacked[4],
            small_stacked[5],
            small_stacked[6],
            small_stacked[7],
            small_stacked[8],
        ),
        ("dp", "tensor"),
    )
    return (
        current,
        grad_rows,
        stacked[0],
        stacked[1],
        stacked[2],
        stacked[3],
        stacked[4],
        stacked[5],
        head_sums[0],
        head_sums[1],
        head_sums[2],
        row_sums[0],
        row_sums[1],
        row_sums[2],
        row_sums[3],
        row_sums[4],
        row_sums[5],
    )


def solution(mesh):
    placed = (
        P(("dp", "tensor"), None),
        P(("dp", "tensor"), None),
        P("dp"),
        P("dp"),
        P(None, "dp", "tensor"),
        P(None, "dp", "tensor"),
        P(None, "dp", "tensor"),
        P(None, "tensor", "dp"),
        P(None, "dp", "tensor"),
        P(None, "tensor", "dp"),
        P(None, "tensor"),
        P(None, "tensor"),
        P(None, "tensor"),
        P(),
        P(),
        P(),
        P(),
        P(),
        P(),
    )
    return jax.shard_map(
        on_device,
        mesh=mesh,
        in_specs=placed,
        out_specs=(
            P(("dp", "tensor"), None),
            P(("dp", "tensor"), None),
            P(None, "dp", "tensor"),
            P(None, "dp", "tensor"),
            P(None, "dp", "tensor"),
            P(None, "tensor", "dp"),
            P(None, "dp", "tensor"),
            P(None, "tensor", "dp"),
            P(None, "tensor"),
            P(None, "tensor"),
            P(None, "tensor"),
            P(),
            P(),
            P(),
            P(),
            P(),
            P(),
        ),
        check_vma=False,
    )
```

profile of v0, /device:TPU:1, one launch (start us, length us, event | category | flops | bytes accessed | tf_op | source)
XLA Modules:
  0.0 2101.7 jit_solution(11126254373600129859)
XLA Ops:
  10.2 22.3 %all-gather.3 = bf16[1,128,1024]{1,2,0:T(8,128)(2,1)S(1)} all-gather(bf16[1,128,64]{1,2,0:T(8,128)(2,1)S(1)} %get-tuple-element.660), channel_id=5, replica_groups=mesh['dp'=16,'tensor'=8] {'dp'}, dimensions={2}, use_global_device_ids=true | all-gather | bytes 278528 | tf_op jit(solution)/shard_map/all_gather | solution.py:170
  33.3 17.1 all-gather.2
  51.2 18.6 all-gather.1
  70.6 17.0 all-gather
  96.3 8.5 while.54
  109.7 81.8 %reduce-scatter.33.cloned.1.call-done = f32[128,1024]{1,0:T(8,128)} async-done(((f32[1024,1024]{1,0:T(8,128)}), f32[128,1024]{1,0:T(8,128)}) %reduce-scatter.33.cloned.1.call-update) | async-done | bytes 524304 | tf_op jit(solution)/shard_map/reduce_scatter | solution.py:154
  194.9 52.3 %all-gather.27.cloned.1.call-done = bf16[1024,1024]{1,0:T(8,128)(2,1)} async-done(((bf16[128,1024]{1,0:T(8,128)(2,1)}), bf16[1024,1024]{1,0:T(8,128)(2,1)}) %all-gather.27.cloned.1.call-update) | async-done | bytes 2097168 | tf_op jit(solution)/shard_map/all_gather | solution.py:151
  247.2 8.5 multiply_convert_fusion.1
  255.7 26.9 %all-gather.43.cloned.1.call-done = bf16[1,512,1024]{1,2,0:T(8,128)(2,1)} async-done(((bf16[1,512,64]{1,2,0:T(8,128)(2,1)}), bf16[1,512,1024]{1,2,0:T(8,128)(2,1)}) %all-gather.43.cloned.1.call-update) | async-done | bytes 1048592 | tf_op jit(solution)/shard_map/all_gather | solution.py:172
  282.6 4.5 fusion.118
  287.8 82.4 %reduce-scatter.35.cloned.1.call-done = f32[128,1024]{1,0:T(8,128)} async-done(((f32[1024,1024]{1,0:T(8,128)}), f32[128,1024]{1,0:T(8,128)}) %reduce-scatter.35.cloned.1.call-update) | async-done | bytes 524304 | tf_op jit(solution)/shard_map/reduce_scatter | solution.py:154
  372.7 22.8 %all-gather.9 = bf16[1,128,1024]{1,2,0:T(8,128)(2,1)} all-gather(bf16[1,128,64]{1,2,0:T(8,128)(2,1)S(1)} %get-tuple-element.659), channel_id=11, replica_groups=mesh['dp'=16,'tensor'=8] {'dp'}, dimensions={2}, use_global_device_ids=true | all-gather | bytes 278528 | tf_op jit(solution)/shard_map/all_gather | solution.py:170
  395.5 18.6 all-gather.8
  414.0 18.5 all-gather.7
  432.5 17.0 all-gather.6
  457.7 8.5 while.55
  470.1 80.5 %reduce-scatter.37.cloned.1.call-done = f32[128,1024]{1,0:T(8,128)} async-done(((f32[1024,1024]{1,0:T(8,128)}), f32[128,1024]{1,0:T(8,128)}) %reduce-scatter.37.cloned.1.call-update) | async-done | bytes 524304 | tf_op jit(solution)/shard_map/reduce_scatter | solution.py:154
  554.1 52.3 %all-gather.31.cloned.1.call-done = bf16[1024,1024]{1,0:T(8,128)(2,1)} async-done(((bf16[128,1024]{1,0:T(8,128)(2,1)}), bf16[1024,1024]{1,0:T(8,128)(2,1)}) %all-gather.31.cloned.1.call-update) | async-done | bytes 2097168 | tf_op jit(solution)/shard_map/all_gather | solution.py:151
  606.4 8.5 multiply_convert_fusion
  614.9 26.9 %all-gather.47.cloned.1.call-done = bf16[1,512,1024]{1,2,0:T(8,128)(2,1)} async-done(((bf16[1,512,64]{1,2,0:T(8,128)(2,1)}), bf16[1,512,1024]{1,2,0:T(8,128)(2,1)}) %all-gather.47.cloned.1.call-update) | async-done | bytes 1048592 | tf_op jit(solution)/shard_map/all_gather | solution.py:172
  641.7 4.5 fusion.108
  646.3 83.0 %reduce-scatter.39.cloned.1.call-done = f32[128,1024]{1,0:T(8,128)} async-done(((f32[1024,1024]{1,0:T(8,128)}), f32[128,1024]{1,0:T(8,128)}) %reduce-scatter.39.cloned.1.call-update) | async-done | bytes 524304 | tf_op jit(solution)/shard_map/reduce_scatter | solution.py:154
  734.2 53.9 %all-gather.33.cloned.1.call-done = bf16[1024,1024]{1,0:T(8,128)(2,1)} async-done(((bf16[128,1024]{1,0:T(8,128)(2,1)}), bf16[1024,1024]{1,0:T(8,128)(2,1)}) %all-gather.33.cloned.1.call-update) | async-done | bytes 2097168 | tf_op jit(solution)/shard_map/all_gather | solution.py:157
  788.0 5.8 convert_reduce_fusion
  798.1 83.9 %reduce-scatter.41.cloned.1.call-done = f32[128,1024]{1,0:T(8,128)} async-done(((f32[1024,1024]{1,0:T(8,128)}), f32[128,1024]{1,0:T(8,128)}) %reduce-scatter.41.cloned.1.call-update) | async-done | bytes 524304 | tf_op jit(solution)/shard_map/reduce_scatter | solution.py:160
  884.8 53.1 %all-gather.35.cloned.1.call-done = bf16[1024,1024]{1,0:T(8,128)(2,1)} async-done(((bf16[128,1024]{1,0:T(8,128)(2,1)}), bf16[1024,1024]{1,0:T(8,128)(2,1)}) %all-gather.35.cloned.1.call-update) | async-done | bytes 2097168 | tf_op jit(solution)/shard_map/all_gather | solution.py:157
  941.5 15.1 while.56
  962.8 83.6 %reduce-scatter.43.cloned.1.call-done = f32[128,1024]{1,0:T(8,128)} async-done(((f32[1024,1024]{1,0:T(8,128)}), f32[128,1024]{1,0:T(8,128)}) %reduce-scatter.43.cloned.1.call-update) | async-done | bytes 524304 | tf_op jit(solution)/shard_map/reduce_scatter | solution.py:160
  1049.0 53.8 %all-gather.37.cloned.1.call-done = bf16[1024,1024]{1,0:T(8,128)(2,1)} async-done(((bf16[128,1024]{1,0:T(8,128)(2,1)}), bf16[1024,1024]{1,0:T(8,128)(2,1)}) %all-gather.37.cloned.1.call-update) | async-done | bytes 2097168 | tf_op jit(solution)/shard_map/all_gather | solution.py:157
  1102.8 4.9 convert_reduce_fusion.1
  1112.2 83.7 %reduce-scatter.45.cloned.1.call-done = f32[128,1024]{1,0:T(8,128)} async-done(((f32[1024,1024]{1,0:T(8,128)}), f32[128,1024]{1,0:T(8,128)}) %reduce-scatter.45.cloned.1.call-update) | async-done | bytes 524304 | tf_op jit(solution)/shard_map/reduce_scatter | solution.py:160
  1205.8 4.3 fusion.185
  1225.6 26.9 %all-gather.39.cloned.1.call-done = bf16[1024,1024]{1,0:T(8,128)(2,1)} async-done(((bf16[128,1024]{1,0:T(8,128)(2,1)}), bf16[1024,1024]{1,0:T(8,128)(2,1)}) %all-gather.39.cloned.1.call-update) | async-done | bytes 2097168 | tf_op jit(solution)/shard_map/all_gather | solution.py:157
  1256.2 15.2 while.57
  1292.7 19.5 reduce-scatter.71.cloned.1.call-done
  1313.1 60.6 %reduce-scatter.63.cloned.1.call-done = f32[64,128]{1,0:T(8,128)} async-done(((f32[1024,128]{1,0:T(8,128)}), f32[64,128]{1,0:T(8,128)}) %reduce-scatter.63.cloned.1.call-update) | async-done | bytes 32784
  1374.5 60.7 %reduce-scatter.67.cloned.1.call-done = f32[64,128]{1,0:T(8,128)} async-done(((f32[1024,128]{1,0:T(8,128)}), f32[64,128]{1,0:T(8,128)}) %reduce-scatter.67.cloned.1.call-update) | async-done | bytes 32784
  1436.1 64.1 %reduce-scatter.55.cloned.1.call-done = f32[64,512]{1,0:T(8,128)} async-done(((f32[1024,512]{1,0:T(8,128)}), f32[64,512]{1,0:T(8,128)}) %reduce-scatter.55.cloned.1.call-update) | async-done | bytes 131088 | tf_op jit(solution)/shard_map/reduce_scatter | solution.py:302
  1500.2 64.8 %reduce-scatter.53.cloned.1.call-done = f32[64,512]{1,0:T(8,128)} async-done(((f32[1024,512]{1,0:T(8,128)}), f32[64,512]{1,0:T(8,128)}) %reduce-scatter.53.cloned.1.call-update) | async-done | bytes 131088 | tf_op jit(solution)/shard_map/reduce_scatter | solution.py:302
  1566.7 63.0 %reduce-scatter.59.cloned.1.call-done = f32[512,64]{0,1:T(8,128)} async-done(((f32[512,1024]{0,1:T(8,128)}), f32[512,64]{0,1:T(8,128)}) %reduce-scatter.59.cloned.1.call-update) | async-done | bytes 131088 | tf_op jit(solution)/shard_map/reduce_scatter | solution.py:303
  1629.7 64.9 %reduce-scatter.57.cloned.1.call-done = f32[512,64]{0,1:T(8,128)} async-done(((f32[512,1024]{0,1:T(8,128)}), f32[512,64]{0,1:T(8,128)}) %reduce-scatter.57.cloned.1.call-update) | async-done | bytes 131088 | tf_op jit(solution)/shard_map/reduce_scatter | solution.py:303
  1696.3 68.6 %all-reduce = (f32[2,1024]{1,0:T(2,128)}, f32[2,1024]{1,0:T(2,128)}, f32[2,1024]{1,0:T(2,128)}, f32[2,1024]{1,0:T(2,128)}, f32[2,1024]{1,0:T(2,128)}, /*index=5*/f32[2,1024]{1,0:T(2,128)}) all-reduce(f32[2,1024]{1,0:T(2,128)S(1)} %get-tuple-element.693, ...), channel_id=1, replica_groups=mesh['dp'=16,'tensor'=8] {'dp','tensor'}, use_global_device_ids=true, to_apply=%region_61.62 | all-reduce | flops 12288 | bytes 98304 | tf_op jit(solution)/shard_map/psum | solution.py:313
  1765.3 28.5 %all-reduce.1 = (f32[2,128]{1,0:T(2,128)}, f32[2,128]{1,0:T(2,128)}, f32[2,512]{1,0:T(2,128)}) all-reduce(f32[2,128]{1,0:T(2,128)S(1)} %get-tuple-element.691, f32[2,128]{1,0:T(2,128)S(1)} %get-tuple-element.692, f32[2,512]{1,0:T(2,128)S(1)} %pad_maximum_fusion.12), channel_id=1, replica_groups=mesh['dp'=16,'tensor'=8] {'dp'}, use_global_device_ids=true, to_apply=%region_52.53 | all-reduce | flops 1536 | bytes 12288 | tf_op jit(solution)/shard_map/psum | solution.py:312
  1795.3 22.1 %reduce-scatter.65.cloned.1.call-done = f32[64,128]{1,0:T(8,128)} async-done(((f32[1024,128]{1,0:T(8,128)}), f32[64,128]{1,0:T(8,128)}) %reduce-scatter.65.cloned.1.call-update) | async-done | bytes 32784
  1819.0 59.9 %reduce-scatter.61.cloned.1.call-done = f32[64,128]{1,0:T(8,128)} async-done(((f32[1024,128]{1,0:T(8,128)}), f32[64,128]{1,0:T(8,128)}) %reduce-scatter.61.cloned.1.call-update) | async-done | bytes 32784
  1880.5 60.4 %reduce-scatter.51.cloned.1.call-done = f32[128,64]{0,1:T(8,128)} async-done(((f32[128,1024]{0,1:T(8,128)}), f32[128,64]{0,1:T(8,128)}) %reduce-scatter.51.cloned.1.call-update) | async-done | bytes 32784 | tf_op jit(solution)/shard_map/reduce_scatter | solution.py:301
  1940.9 61.5 %reduce-scatter.49.cloned.1.call-done = f32[128,64]{0,1:T(8,128)} async-done(((f32[128,1024]{0,1:T(8,128)}), f32[128,64]{0,1:T(8,128)}) %reduce-scatter.49.cloned.1.call-update) | async-done | bytes 32784 | tf_op jit(solution)/shard_map/reduce_scatter | solution.py:301
  2003.8 88.1 %reduce-scatter.47.cloned.1.call-done = f32[128,1024]{1,0:T(8,128)} async-done(((f32[1024,1024]{1,0:T(8,128)}), f32[128,1024]{1,0:T(8,128)}) %reduce-scatter.47.cloned.1.call-update) | async-done | bytes 524304 | tf_op jit(solution)/shard_map/reduce_scatter | solution.py:160
  (477 shorter events, 179.2 us)
Async XLA Ops:
  8.0 81.0 %all-gather.25.cloned.1.call-start = ((), (), s32[]{:S(2)}) async-start(), calls=%async_computation.20 | async-start | bytes 2359296 | tf_op jit(solution)/shard_map/all_gather | solution.py:151
  8.8 182.7 %reduce-scatter.33.cloned.1.call-start = ((), (), s32[]{:S(2)}) async-start(), calls=%async_computation.21 | async-start | bytes 4718592 | tf_op jit(solution)/shard_map/reduce_scatter | solution.py:154
  108.0 85.9 %copy-start.52 = (bf16[2,512,64]{1,2,0:T(8,128)(2,1)S(1)}, bf16[2,512,64]{1,2,0:T(8,128)(2,1)}, u32[]{:S(2)}) copy-start(bf16[2,512,64]{1,2,0:T(8,128)(2,1)} %param.36) | copy-start | bytes 393220
  108.0 86.8 %copy-start.70 = (f32[2,512]{1,0:T(2,128)S(1)}, f32[2,512]{1,0:T(2,128)}, u32[]{:S(2)}) copy-start(f32[2,512]{1,0:T(2,128)} %param.39) | copy-start | bytes 12292
  108.0 86.9 %all-gather.41.cloned.1.call-start = ((), (), s32[]{:S(2)}) async-start(), calls=%async_computation.42 | async-start | bytes 1114112 | tf_op jit(solution)/shard_map/all_gather | solution.py:171
  109.5 137.7 %all-gather.27.cloned.1.call-start = ((), (), s32[]{:S(2)}) async-start(), calls=%async_computation.22 | async-start | bytes 2359296 | tf_op jit(solution)/shard_map/all_gather | solution.py:151
  109.6 260.5 %copy-start.53 = (f32[1,1024]{1,0:T(1,128)}, f32[1,1024]{1,0:T(1,128)S(1)}, u32[]{:S(2)}) copy-start(f32[1,1024]{1,0:T(1,128)S(1)} %get-tuple-element.672) | copy-start | bytes 12292
  192.7 177.5 %copy-start.6 = (f32[128,1024]{1,0:T(8,128)}, f32[128,1024]{1,0:T(8,128)S(1)}, u32[]{:S(2)}) copy-start(f32[128,1024]{1,0:T(8,128)S(1)} %get-tuple-element.645) | copy-start | bytes 1572868
  192.7 177.5 %copy-start.60 = (f32[128]{0:T(128)}, f32[128]{0:T(128)S(1)}, u32[]{:S(2)}) copy-start(f32[128]{0:T(128)S(1)} %broadcast_multiply_fusion.3) | copy-start | bytes 1540
  192.9 177.2 %copy-start.62 = (f32[128]{0:T(128)}, f32[128]{0:T(128)S(1)}, u32[]{:S(2)}) copy-start(f32[128]{0:T(128)S(1)} %fusion.155) | copy-start | bytes 1540
  193.8 88.7 %all-gather.43.cloned.1.call-start = ((), (), s32[]{:S(2)}) async-start(), calls=%async_computation.43 | async-start | bytes 1114112 | tf_op jit(solution)/shard_map/all_gather | solution.py:172
  194.6 175.6 %reduce-scatter.35.cloned.1.call-start = ((), (), s32[]{:S(2)}) async-start(), calls=%async_computation.23 | async-start | bytes 4718592 | tf_op jit(solution)/shard_map/reduce_scatter | solution.py:154
  287.1 162.4 %all-gather.29.cloned.1.call-start = ((), (), s32[]{:S(2)}) async-start(), calls=%async_computation.24 | async-start | bytes 2359296 | tf_op jit(solution)/shard_map/all_gather | solution.py:151
  372.6 177.9 %reduce-scatter.37.cloned.1.call-start = ((), (), s32[]{:S(2)}) async-start(), calls=%async_computation.25 | async-start | bytes 4718592 | tf_op jit(solution)/shard_map/reduce_scatter | solution.py:154
  469.3 84.8 %all-gather.45.cloned.1.call-start = ((), (), s32[]{:S(2)}) async-start(), calls=%async_computation.44 | async-start | bytes 1114112 | tf_op jit(solution)/shard_map/all_gather | solution.py:171
  470.0 136.4 %all-gather.31.cloned.1.call-start = ((), (), s32[]{:S(2)}) async-start(), calls=%async_computation.26 | async-start | bytes 2359296 | tf_op jit(solution)/shard_map/all_gather | solution.py:151
  553.0 88.7 %all-gather.47.cloned.1.call-start = ((), (), s32[]{:S(2)}) async-start(), calls=%async_computation.45 | async-start | bytes 1114112 | tf_op jit(solution)/shard_map/all_gather | solution.py:172
  553.6 175.7 %reduce-scatter.39.cloned.1.call-start = ((), (), s32[]{:S(2)}) async-start(), calls=%async_computation.27 | async-start | bytes 4718592 | tf_op jit(solution)/shard_map/reduce_scatter | solution.py:154
  646.2 84.6 %copy-start.39 = (bf16[128,1024]{1,0:T(8,128)(2,1)S(1)}, bf16[128,1024]{1,0:T(8,128)(2,1)}, u32[]{:S(2)}) copy-start(bf16[128,1024]{1,0:T(8,128)(2,1)} %param.28) | copy-start | bytes 786436
  646.2 141.8 %all-gather.33.cloned.1.call-start = ((), (), s32[]{:S(2)}) async-start(), calls=%async_computation.28 | async-start | bytes 2359296 | tf_op jit(solution)/shard_map/all_gather | solution.py:157
  734.1 147.9 %reduce-scatter.41.cloned.1.call-start = ((), (), s32[]{:S(2)}) async-start(), calls=%async_computation.29 | async-start | bytes 4718592 | tf_op jit(solution)/shard_map/reduce_scatter | solution.py:160
  798.0 139.8 %all-gather.35.cloned.1.call-start = ((), (), s32[]{:S(2)}) async-start(), calls=%async_computation.30 | async-start | bytes 2359296 | tf_op jit(solution)/shard_map/all_gather | solution.py:157
  884.5 161.9 %reduce-scatter.43.cloned.1.call-start = ((), (), s32[]{:S(2)}) async-start(), calls=%async_computation.31 | async-start | bytes 4718592 | tf_op jit(solution)/shard_map/reduce_scatter | solution.py:160
  962.7 140.1 %copy-start.73 = (f32[1,512]{1,0:T(1,128)S(1)}, f32[1,512]{1,0:T(1,128)}, u32[]{:S(2)}) copy-start(f32[1,512]{1,0:T(1,128)} %copy-done.72) | copy-start | bytes 6148
  962.7 140.1 %copy-start.80 = (bf16[1,512,1024]{1,2,0:T(8,128)(2,1)S(1)}, bf16[1,512,1024]{1,2,0:T(8,128)(2,1)}, u32[]{:S(2)}) copy-start(bf16[1,512,1024]{1,2,0:T(8,128)(2,1)} %all-gather.43.cloned.1.call-done) | copy-start | bytes 3145732
  962.7 140.0 %all-gather.37.cloned.1.call-start = ((), (), s32[]{:S(2)}) async-start(), calls=%async_computation.32 | async-start | bytes 2359296 | tf_op jit(solution)/shard_map/all_gather | solution.py:157
  1048.9 147.0 %reduce-scatter.45.cloned.1.call-start = ((), (), s32[]{:S(2)}) async-start(), calls=%async_computation.33 | async-start | bytes 4718592 | tf_op jit(solution)/shard_map/reduce_scatter | solution.py:160
  1111.9 85.4 %copy-start.75 = (f32[128]{0:T(128)S(1)}, f32[128]{0:T(128)}, u32[]{:S(2)}) copy-start(f32[128]{0:T(128)} %copy-done.74) | copy-start | bytes 1540
  1111.9 87.4 %copy-start.3 = (bf16[1024,1024]{1,0:T(8,128)(2,1)S(1)}, bf16[1024,1024]{1,0:T(8,128)(2,1)}, u32[]{:S(2)}) copy-start(bf16[1024,1024]{1,0:T(8,128)(2,1)} %all-gather.29.cloned.1.call-done) | copy-start | bytes 6291460
  1111.9 140.7 %all-gather.39.cloned.1.call-start = ((), (), s32[]{:S(2)}) async-start(), calls=%async_computation.34 | async-start | bytes 2359296 | tf_op jit(solution)/shard_map/all_gather | solution.py:157
  1199.2 113.0 %reduce-scatter.71.cloned.1.call-start = ((), (), s32[]{:S(2)}) async-start(), calls=%async_computation.51 | async-start | bytes 557056
  1202.0 171.6 %reduce-scatter.63.cloned.1.call-start = ((), (), s32[]{:S(2)}) async-start(), calls=%async_computation.47 | async-start | bytes 557056
  1203.9 231.3 %reduce-scatter.67.cloned.1.call-start = ((), (), s32[]{:S(2)}) async-start(), calls=%async_computation.49 | async-start | bytes 557056
  1205.7 294.5 %reduce-scatter.55.cloned.1.call-start = ((), (), s32[]{:S(2)}) async-start(), calls=%async_computation.39 | async-start | bytes 2228224 | tf_op jit(solution)/shard_map/reduce_scatter | solution.py:302
  1210.1 354.9 %reduce-scatter.53.cloned.1.call-start = ((), (), s32[]{:S(2)}) async-start(), calls=%async_computation.38 | async-start | bytes 2228224 | tf_op jit(solution)/shard_map/reduce_scatter | solution.py:302
  1215.7 414.0 %reduce-scatter.59.cloned.1.call-start = ((), (), s32[]{:S(2)}) async-start(), calls=%async_computation.41 | async-start | bytes 2228224 | tf_op jit(solution)/shard_map/reduce_scatter | solution.py:303
  1219.9 474.7 %reduce-scatter.57.cloned.1.call-start = ((), (), s32[]{:S(2)}) async-start(), calls=%async_computation.40 | async-start | bytes 2228224 | tf_op jit(solution)/shard_map/reduce_scatter | solution.py:303
  1225.3 568.4 %reduce-scatter.69.cloned.1.call-start = ((), (), s32[]{:S(2)}) async-start(), calls=%async_computation.50 | async-start | bytes 557056
  1276.0 541.5 %reduce-scatter.65.cloned.1.call-start = ((), (), s32[]{:S(2)}) async-start(), calls=%async_computation.48 | async-start | bytes 557056
  1277.6 601.4 %reduce-scatter.61.cloned.1.call-start = ((), (), s32[]{:S(2)}) async-start(), calls=%async_computation.46 | async-start | bytes 557056
  1281.3 659.6 %reduce-scatter.51.cloned.1.call-start = ((), (), s32[]{:S(2)}) async-start(), calls=%async_computation.37 | async-start | bytes 557056 | tf_op jit(solution)/shard_map/reduce_scatter | solution.py:301
  1284.8 717.5 %reduce-scatter.49.cloned.1.call-start = ((), (), s32[]{:S(2)}) async-start(), calls=%async_computation.36 | async-start | bytes 557056 | tf_op jit(solution)/shard_map/reduce_scatter | solution.py:301
  1286.7 805.1 %reduce-scatter.47.cloned.1.call-start = ((), (), s32[]{:S(2)}) async-start(), calls=%async_computation.35 | async-start | bytes 4718592 | tf_op jit(solution)/shard_map/reduce_scatter | solution.py:160
  1291.5 144.6 %copy-start.58 = (f32[1024]{0:T(1024)S(1)}, f32[1024]{0:T(1024)}, u32[]{:S(2)}) copy-start(f32[1024]{0:T(1024)} %get-tuple-element.512) | copy-start | bytes 12292
  1291.5 144.6 %copy-start.59 = (f32[1024]{0:T(1024)S(1)}, f32[1024]{0:T(1024)}, u32[]{:S(2)}) copy-start(f32[1024]{0:T(1024)} %get-tuple-element.517) | copy-start | bytes 12292
  1291.5 144.6 %copy-start.71 = (f32[512]{0:T(512)S(1)}, f32[512]{0:T(512)}, u32[]{:S(2)}) copy-start(f32[512]{0:T(512)} %get-tuple-element.687) | copy-start | bytes 6148
  1291.5 404.8 %copy-start.57 = (f32[1024]{0:T(1024)S(1)}, f32[1024]{0:T(1024)}, u32[]{:S(2)}) copy-start(f32[1024]{0:T(1024)} %get-tuple-element.613) | copy-start | bytes 12292
  1292.4 799.4 %copy-start.12 = (f32[128,1024]{1,0:T(8,128)S(1)}, f32[128,1024]{1,0:T(8,128)}, u32[]{:S(2)}) copy-start(f32[128,1024]{1,0:T(8,128)} %copy-done.11) | copy-start | bytes 1572868
  (82 other events, 958.0 us)
Sparse Core Ops, SparseCore 0:
  11.2 58.2 all-gather.24
  108.1 83.3 reduce-scatter.32
  372.7 55.3 all-gather.28
  469.4 81.1 reduce-scatter.36
  734.3 53.7 all-gather.32
  798.2 83.8 reduce-scatter.40
  1049.0 53.6 all-gather.36
  1112.0 83.8 reduce-scatter.44
Sparse Core Ops, SparseCore 1:
  110.8 36.9 all-gather.40
  193.9 53.2 all-gather.26
  249.4 33.2 all-gather.42
  287.2 82.9 reduce-scatter.34
  472.3 33.6 all-gather.44
  553.1 53.2 all-gather.30
  608.5 33.2 all-gather.46
  646.3 82.9 reduce-scatter.38
  884.6 53.2 all-gather.34
  962.8 83.6 reduce-scatter.42
  1199.3 53.2 all-gather.38
  1255.0 57.2 reduce-scatter.70
  1314.6 59.0 reduce-scatter.62
  1376.0 59.1 reduce-scatter.66
  1437.7 62.4 reduce-scatter.54
  1502.7 62.3 reduce-scatter.52
  1567.6 62.1 reduce-scatter.58
  1632.2 62.3 reduce-scatter.56
  1696.9 58.9 reduce-scatter.68
  1758.3 59.1 reduce-scatter.64
  1819.8 59.1 reduce-scatter.60
  1881.7 59.1 reduce-scatter.50
  1943.2 59.1 reduce-scatter.48
  2006.3 85.5 reduce-scatter.46
where the time goes:
time: 2110 us; the launch traced here: 2100 us
  waiting for transfers between devices  1620 us (77%)
  blocking collectives  249 us (12%)
  matrix products  132 us (6%)
  other arithmetic  41.4 us (2%)
  local copies, waits for them, and re-layouts  40.9 us (2%)
    reduce_scatter x4, waiting for transfers between devices, sum_grads(): lax.psum_scatter(partial_value, 'tensor', scatter_dimension=0, tiled=True)  339 us
    reduce_scatter x4, waiting for transfers between devices, sum_heads(): lax.psum_scatter(partial_value, 'tensor', scatter_dimension=0, tiled=True)  328 us
    unnamed x38, waiting for transfers between devices  225 us
    all_gather x4, waiting for transfers between devices, gather_grads(): return lax.all_gather(rows, 'tensor', axis=0, tiled=True)  188 us
    reduce_scatter x2, waiting for transfers between devices, on_device(): lax.psum_scatter(mat_terms[4], 'dp', scatter_dimension=0, tiled=True)  129 us
    reduce_scatter x2, waiting for transfers between devices, on_device(): lax.psum_scatter(mat_terms[5], 'dp', scatter_dimension=1, tiled=True)  128 us
    reduce_scatter x2, waiting for transfers between devices, on_device(): lax.psum_scatter(mat_terms[3], 'dp', scatter_dimension=1, tiled=True)  122 us
    all_gather x4, waiting for transfers between devices, gather_rows(): return lax.all_gather(rows, 'tensor', axis=0, tiled=True)  105 us
  transfers between devices with their start and end apart: 32, of which 27 were waited for; matrix products, arithmetic and copies ran while one was open for 5% of the time, Pallas kernels for 0%

commit v1 on v0

v1 whole, which is shorter than its diff:
```python
import jax
import jax.numpy as jnp
from jax import lax
from jax.sharding import Mesh, PartitionSpec as P

HEAD_DIM = 64
NORM_EPS = 1e-12
MASKED = -1000000000.0
F32 = jnp.float32
BF16 = jnp.bfloat16

AXES = ("y", "zl", "c", "zh", "x")
DP = ("y", "zl", "c")
TENSOR = ("zh", "x")
OWNERS = ("y", "zl", "zh")
HOPS = (0, 1, 3, 2)
ORDER = (2, 1, 3, 0)


def dot(left, right, left_dim, right_dim):
    return lax.dot_general(
        left, right, (((left_dim,), (right_dim,)), ((), ())), preferred_element_type=F32
    )


def along_x(value, hop):
    ring = lax.axis_size("x")
    return lax.ppermute(value, "x", [(i, (i + hop) % ring) for i in range(ring)])


def other_core(value):
    return lax.ppermute(value, "c", [(0, 1), (1, 0)])


def swap_core_z(value):
    ring = lax.axis_size("x")
    pairs = []
    for core in range(2):
        for high in range(2):
            for x in range(ring):
                pairs.append(((core * 2 + high) * ring + x, (high * 2 + core) * ring + x))
    return lax.ppermute(value, ("c", "zh", "x"), pairs)


def gather_pairs(rows):
    chunks = {}
    for hop in (1, 3, 2, 0):
        mine = along_x(rows, hop) if hop else rows
        chunks[hop] = jnp.concatenate([mine, other_core(mine)], axis=0)
    return chunks


def scatter_pairs(parts):
    total = None
    for hop in ORDER:
        part = parts[hop]
        half = part.shape[0] // 2
        both = part[:half] + other_core(part[half:].astype(BF16)).astype(F32)
        if hop:
            both = along_x(both.astype(BF16), -hop).astype(F32)
        total = both if total is None else total + both
    return total


def normalized(rows):
    center = rows - jnp.mean(rows, axis=-1, keepdims=True)
    spread = jnp.mean(center * center, axis=-1, keepdims=True)
    scale = lax.rsqrt(spread + NORM_EPS)
    return center * scale, scale


def norm_back(grad, unit, scale, gain):
    gain_grad = jnp.sum(grad * unit, axis=0)
    shift_grad = jnp.sum(grad, axis=0)
    scaled = grad * gain
    mean_all = jnp.mean(scaled, axis=-1, keepdims=True)
    mean_unit = jnp.mean(scaled * unit, axis=-1, keepdims=True)
    return scale * (scaled - mean_all - unit * mean_unit), gain_grad, shift_grad


def gelu_exact(values):
    return jax.nn.gelu(values, approximate=False)


def attend(queries, keys, values, allowed):
    mixed, kept = [], []
    for head in range(queries.shape[1] // HEAD_DIM):
        cols = slice(head * HEAD_DIM, (head + 1) * HEAD_DIM)
        scores = dot(queries[:, cols], keys[:, cols], 1, 1) * HEAD_DIM**-0.5
        scores = jnp.where(allowed, scores, MASKED)
        exps = jnp.exp(scores - jnp.max(scores, axis=-1, keepdims=True))
        soft = (exps / jnp.sum(exps, axis=-1, keepdims=True)).astype(BF16)
        kept.append(soft)
        mixed.append(dot(soft, values[:, cols], 1, 0).astype(BF16))
    return jnp.concatenate(mixed, axis=1), kept


def attend_chunk_back(queries, keys, values, kept, grads):
    grad_q, grad_k, grad_v = [], [], []
    for head in range(queries.shape[1] // HEAD_DIM):
        cols = slice(head * HEAD_DIM, (head + 1) * HEAD_DIM)
        soft = kept[head]
        wide = soft.astype(F32)
        grad_soft = dot(grads[:, cols], values[:, cols], 1, 1).astype(BF16).astype(F32)
        row = jnp.sum(grad_soft * wide, axis=-1, keepdims=True)
        grad_scores = (wide * (grad_soft - row)).astype(BF16)
        grad_q.append(dot(grad_scores, keys[:, cols], 1, 0) * HEAD_DIM**-0.5)
        grad_k.append(dot(grad_scores, queries[:, cols], 0, 0))
        grad_v.append(dot(soft, grads[:, cols], 0, 0))
    return (
        jnp.concatenate(grad_q, axis=1).astype(BF16),
        jnp.concatenate(grad_k, axis=1),
        jnp.concatenate(grad_v, axis=1),
    )


def stack_chunks(chunks):
    return jnp.concatenate([chunks[hop] for hop in HOPS], axis=0)


def on_device(
    layer_input,
    cotangent,
    segment,
    live_mask,
    query_weight,
    key_weight,
    value_weight,
    out_weight,
    up_weight,
    down_weight,
    query_bias,
    value_bias,
    up_bias,
    out_bias,
    down_bias,
    attention_gain,
    attention_shift,
    output_gain,
    output_shift,
):
    layers = query_weight.shape[0]
    core, high, x = lax.axis_index("c"), lax.axis_index("zh"), lax.axis_index("x")
    ring = lax.axis_size("x")
    owners = 16
    rows_in = swap_core_z(layer_input)

    attn_shards = jnp.concatenate(
        [query_weight, key_weight, value_weight, jnp.swapaxes(out_weight, 1, 2)], axis=2
    )
    ffn_shards = jnp.concatenate([up_weight, jnp.swapaxes(down_weight, 1, 2)], axis=2)
    shard_rows, attn_cols = attn_shards.shape[1:]
    ffn_cols = ffn_shards.shape[2]
    width = shard_rows * owners
    attn_shards = swap_core_z(attn_shards)
    ffn_shards = swap_core_z(ffn_shards)
    first = jnp.broadcast_to(attn_shards[0], (owners, shard_rows, attn_cols))
    attn_mats = [lax.all_to_all(first, OWNERS, 0, 0, tiled=True).reshape(width, attn_cols)]
    ffn_mats = [lax.all_gather(ffn_shards[0], OWNERS, axis=0, tiled=True)]
    for layer in range(1, layers):
        attn_mats.append(lax.all_gather(attn_shards[layer], OWNERS, axis=0, tiled=True))
        ffn_mats.append(lax.all_gather(ffn_shards[layer], OWNERS, axis=0, tiled=True))
    qkv_cols = 3 * attn_cols // 4
    head_cols = attn_cols // 4
    ffn_half = ffn_cols // 2

    biases = jnp.concatenate([query_bias, value_bias, up_bias], axis=1)
    biases = swap_core_z(biases)
    query_bias = biases[:, :head_cols]
    value_bias = biases[:, head_cols : 2 * head_cols]
    up_bias = biases[:, 2 * head_cols :]

    packed = (segment * 2 + live_mask).astype(F32)
    packed = jnp.where(core == high, packed, other_core(packed)).reshape(2, ring, -1)
    packed = jnp.where(core == 0, packed, packed[::-1])
    ordered = []
    for hop in HOPS:
        ordered.append(lax.dynamic_index_in_dim(packed, lax.rem(x + ring - hop, ring), 1, False))
    marks = jnp.stack(ordered).reshape(len(HOPS), -1)
    seg_chunks = jnp.floor(marks * 0.5)
    live = (marks - 2 * seg_chunks).reshape(-1)
    key_mark = jnp.where(live > 0.5, seg_chunks.reshape(-1), -1.0)
    allowed = {
        hop: seg_chunks[index][:, None] == key_mark[None, :] for index, hop in enumerate(HOPS)
    }

    current = rows_in.astype(F32)
    saved = []
    for layer in range(layers):
        qkv_mat = attn_mats[layer][:, :qkv_cols]
        out_mat = attn_mats[layer][:, qkv_cols:]
        up_mat = ffn_mats[layer][:, :ffn_half]
        down_mat = ffn_mats[layer][:, ffn_half:]
        qkv_bias = jnp.concatenate(
            [query_bias[layer], jnp.zeros_like(query_bias[layer]), value_bias[layer]]
        )
        inputs = gather_pairs(current.astype(BF16))
        qkv = {hop: (dot(inputs[hop], qkv_mat, 1, 0) + qkv_bias).astype(BF16) for hop in HOPS}
        keys = stack_chunks({hop: qkv[hop][:, head_cols : 2 * head_cols] for hop in HOPS})
        values = stack_chunks({hop: qkv[hop][:, 2 * head_cols :] for hop in HOPS})
        attended, soft, parts = {}, {}, {}
        for hop in ORDER:
            attended[hop], soft[hop] = attend(
                qkv[hop][:, :head_cols], keys, values, allowed[hop]
            )
            parts[hop] = dot(attended[hop], out_mat, 1, 1)
        first_sum = current + scatter_pairs(parts) + out_bias[layer]
        mid_unit, mid_scale = normalized(first_sum)
        normed_mid = mid_unit * attention_gain[layer] + attention_shift[layer]
        mids = gather_pairs(normed_mid.astype(BF16))
        pre_gelu, activated, parts = {}, {}, {}
        for hop in ORDER:
            pre_gelu[hop] = dot(mids[hop], up_mat, 1, 0) + up_bias[layer]
            activated[hop] = gelu_exact(pre_gelu[hop]).astype(BF16)
            parts[hop] = dot(activated[hop], down_mat, 1, 1)
        second_sum = normed_mid + scatter_pairs(parts) + down_bias[layer]
        out_unit, out_scale = normalized(second_sum)
        current = out_unit * output_gain[layer] + output_shift[layer]
        saved.append(
            (inputs, qkv, keys, values, attended, soft, mid_unit, mid_scale, mids, pre_gelu,
             activated, out_unit, out_scale)
        )
    layer_output = swap_core_z(current.astype(BF16)).astype(F32)

    grad_rows = swap_core_z(cotangent).astype(F32)
    attn_grads, ffn_grads = [None] * layers, [None] * layers
    head_sums, row_sums = [None] * layers, [None] * layers
    tail = None
    for layer in reversed(range(layers)):
        (inputs, qkv, keys, values, attended, soft, mid_unit, mid_scale, mids, pre_gelu,
         activated, out_unit, out_scale) = saved[layer]
        qkv_mat = attn_mats[layer][:, :qkv_cols]
        out_mat = attn_mats[layer][:, qkv_cols:]
        up_mat = ffn_mats[layer][:, :ffn_half]
        down_mat = ffn_mats[layer][:, ffn_half:]
        grad_second, out_gain_term, out_shift_term = norm_back(
            grad_rows, out_unit, out_scale, output_gain[layer]
        )
        branch_low = grad_second.astype(BF16)
        down_bias_term = jnp.sum(branch_low.astype(F32), axis=0)
        branch = gather_pairs(branch_low)
        grad_pre, parts = {}, {}
        for hop in ORDER:
            grad_act = dot(branch[hop], down_mat, 1, 0)
            grad_pre[hop] = jax.vjp(gelu_exact, pre_gelu[hop])[1](grad_act)[0].astype(BF16)
            parts[hop] = dot(grad_pre[hop], up_mat, 1, 1)
        grad_mid = grad_second + scatter_pairs(parts)
        all_pre = stack_chunks(grad_pre)
        up_bias_term = jnp.sum(all_pre.astype(F32), axis=0)
        up_grad = dot(stack_chunks(mids), all_pre, 0, 0)
        down_grad = dot(stack_chunks(branch), stack_chunks(activated), 0, 0)
        terms = jnp.concatenate([up_grad.astype(BF16), down_grad.astype(BF16)], axis=1)
        ffn_grads[layer] = lax.psum_scatter(terms, OWNERS, scatter_dimension=0, tiled=True).astype(F32)

        grad_first, att_gain_term, att_shift_term = norm_back(
            grad_mid, mid_unit, mid_scale, attention_gain[layer]
        )
        attn_low = grad_first.astype(BF16)
        out_bias_term = jnp.sum(attn_low.astype(F32), axis=0)
        attn_chunks = gather_pairs(attn_low)
        grad_q, grad_k, grad_v = {}, [], []
        for hop in ORDER:
            grad_att = dot(attn_chunks[hop], out_mat, 1, 0).astype(BF16)
            q_rows = qkv[hop][:, :head_cols]
            grad_q[hop], k_term, v_term = attend_chunk_back(
                q_rows, keys, values, soft[hop], grad_att
            )
            grad_k.append(k_term)
            grad_v.append(v_term)
        grad_keys = (sum(grad_k) * HEAD_DIM**-0.5).astype(BF16)
        grad_values = sum(grad_v).astype(BF16)
        grad_qkv = jnp.concatenate([stack_chunks(grad_q), grad_keys, grad_values], axis=1)
        count = grad_qkv.shape[0] // len(HOPS)
        parts = {}
        for index, hop in enumerate(HOPS):
            parts[hop] = dot(grad_qkv[index * count : (index + 1) * count], qkv_mat, 1, 1)
        grad_rows = grad_first + scatter_pairs(parts)
        qkv_grad = dot(stack_chunks(inputs), grad_qkv, 0, 0)
        out_grad = dot(stack_chunks(attn_chunks), stack_chunks(attended), 0, 0)
        terms = jnp.concatenate([qkv_grad.astype(BF16), out_grad.astype(BF16)], axis=1)
        bias_terms = jnp.sum(grad_qkv.astype(F32), axis=0)
        head_sums[layer] = jnp.concatenate(
            [bias_terms[:head_cols], bias_terms[2 * head_cols :], up_bias_term]
        )
        row_sums[layer] = jnp.stack(
            [out_bias_term, down_bias_term, att_gain_term, att_shift_term, out_gain_term,
             out_shift_term]
        )
        if layer > 0:
            attn_grads[layer] = lax.psum_scatter(terms, OWNERS, scatter_dimension=0, tiled=True).astype(F32)
        else:
            tail = terms

    slices = jnp.stack(row_sums).reshape(layers * 6, 2, ring, -1)
    slices = jnp.transpose(slices, (1, 2, 0, 3))
    mine = lax.dynamic_index_in_dim(slices, core, 0, False)
    send = lax.dynamic_index_in_dim(slices, 1 - core, 0, False)
    both = mine + other_core(send)
    kept = None
    for hop in HOPS:
        part = lax.dynamic_index_in_dim(both, lax.rem(x + ring - hop, ring), 0, False)
        part = along_x(part, -hop) if hop else part
        kept = part if kept is None else kept + part
    small = jnp.concatenate([jnp.stack(head_sums).reshape(-1), kept.reshape(-1)])
    small_len = small.shape[0]
    extra = -(-small_len // (16 * attn_cols)) * 16
    small_rows = jnp.pad(small, (0, extra * attn_cols - small_len)).reshape(1, extra, attn_cols)
    sent = jnp.concatenate(
        [
            tail.reshape(owners, shard_rows, attn_cols),
            jnp.broadcast_to(small_rows.astype(BF16), (owners, extra, attn_cols)),
        ],
        axis=1,
    )
    got = lax.all_to_all(sent, OWNERS, 0, 0, tiled=True)
    got = jnp.sum(got.astype(F32), axis=0)
    attn_grads[0] = got[:shard_rows]
    small = got[shard_rows:].reshape(-1)[:small_len]
    head_len = layers * head_sums[0].shape[0]

    grad_all = jnp.concatenate([jnp.stack(attn_grads), jnp.stack(ffn_grads)], axis=2)
    grad_all = swap_core_z(grad_all.astype(BF16)).astype(F32)
    bias_all = swap_core_z(small[:head_len].reshape(layers, -1))
    input_grad = swap_core_z(grad_rows.astype(BF16)).astype(F32)

    piece = small[head_len:].reshape(layers * 6, -1)
    table = jnp.zeros((2, ring) + piece.shape, F32)
    for hop in HOPS:
        one = along_x(piece, hop) if hop else piece
        where = lax.rem(x + ring - hop, ring)
        table = lax.dynamic_update_slice(table, one[None, None], (core, where, 0, 0))
    pair = lax.dynamic_slice_in_dim(table, core, 1, 0)
    table = lax.dynamic_update_slice(table, other_core(pair), (1 - core, 0, 0, 0))
    rows_out = jnp.transpose(table, (2, 0, 1, 3)).reshape(layers, 6, -1)

    def cols(start, count):
        return grad_all[:, :, start : start + count]

    return (
        layer_output,
        input_grad,
        cols(0, head_cols),
        cols(head_cols, head_cols),
        cols(2 * head_cols, head_cols),
        jnp.swapaxes(cols(3 * head_cols, head_cols), 1, 2),
        cols(attn_cols, ffn_half),
        jnp.swapaxes(cols(attn_cols + ffn_half, ffn_half), 1, 2),
        bias_all[:, :head_cols],
        bias_all[:, head_cols : 2 * head_cols],
        bias_all[:, 2 * head_cols :],
        rows_out[:, 0],
        rows_out[:, 1],
        rows_out[:, 2],
        rows_out[:, 3],
        rows_out[:, 4],
        rows_out[:, 5],
    )


def solution(mesh):
    split = Mesh(mesh.devices.reshape(4, 2, 2, 2, 4), AXES)
    rows = P(DP + TENSOR, None)
    tall = P(None, DP, TENSOR)
    wide = P(None, TENSOR, DP)
    held = P(None, TENSOR)
    return jax.shard_map(
        on_device,
        mesh=split,
        in_specs=(rows, rows, P(DP), P(DP), tall, tall, tall, wide, tall, wide, held, held, held)
        + (P(),) * 6,
        out_specs=(rows, rows, tall, tall, tall, wide, tall, wide, held, held, held) + (P(),) * 6,
        check_vma=False,
    )
```

time: 2110 us -> 637 us (0.30)
  waiting for transfers between devices: 1620 us -> 152 us
  blocking collectives: 249 us -> 0 us
  starting transfers between devices: 2.92 us -> 204 us
  local copies, waits for them, and re-layouts: 40.9 us -> 87.4 us
    reduce_scatter x14 -> x1, waiting for transfers between devices: 1050 us -> 0.02 us  [on_device(): lax.psum_scatter(terms, OWNERS, scatter_dimension=0, tiled=True).astype(F32)]
    all_gather x12 -> x3, waiting for transfers between devices: 346 us -> 21.8 us  [the longest x1 12.9 us: on_device(): lax.all_gather(ffn_shards[layer], OWNERS, axis=0, tiled=True)]
    unnamed x38 -> x8, waiting for transfers between devices: 225 us -> 23.5 us
    ppermute x0 -> x130, starting transfers between devices: none -> 194 us  [the longest x67 80.1 us: other_core(): return lax.ppermute(value, 'c', [(0, 1), (1, 0)])]
    all_gather x8 -> x0, blocking collectives: 152 us -> none  [the longest x2 45.1 us: on_device(): lax.all_gather(out_weight[layer], 'dp', axis=1, tiled=True)]
    ppermute x0 -> x130, waiting for transfers between devices: none -> 107 us  [the longest x54 92.6 us: along_x(): lax.ppermute(value, 'x', [(i, (i + hop) % ring) for i in range(ring)])]
    psum x2 -> x0, blocking collectives: 97.1 us -> none  [the longest x1 68.6 us: on_device(): lax.psum((small_stacked[3], small_stacked[4], small_stacked[5], small_sta...]
    unnamed x174 -> x423, local copies, waits for them, and re-layouts: 26 us -> 62 us
  transfers between devices with their start and end apart: 32 -> 138, of which waited for: 27 -> 36; matrix products, arithmetic and copies ran while one was open for 5% -> 38% of each run, Pallas kernels for 0% -> 0%
where the time goes in v1:
time: 637 us; the launch traced here: 626 us
  starting transfers between devices  204 us (32%)
  waiting for transfers between devices  152 us (24%)
  matrix products  120 us (19%)
  local copies, waits for them, and re-layouts  87.4 us (14%)
  other arithmetic  44 us (7%)
  between operations  18.8 us (3%)
    dot_general x168, matrix products, dot(): lax.dot_general(left, right, (((left_dim,), (right_dim,)), ((), ())), pre...  120 us
    ppermute x54, waiting for transfers between devices, along_x(): lax.ppermute(value, 'x', [(i, (i + hop) % ring) for i in range(ring)])  92.6 us
    ppermute x67, starting transfers between devices, other_core(): return lax.ppermute(value, 'c', [(0, 1), (1, 0)])  80.1 us
    ppermute x54, starting transfers between devices, along_x(): lax.ppermute(value, 'x', [(i, (i + hop) % ring) for i in range(ring)])  63.9 us
    unnamed x423, local copies, waits for them, and re-layouts  62 us
    ppermute x9, starting transfers between devices, swap_core_z(): return lax.ppermute(value, ('c', 'zh', 'x'), pairs)  50 us
    unnamed x8, waiting for transfers between devices  23.5 us
    ppermute x9, waiting for transfers between devices, swap_core_z(): return lax.ppermute(value, ('c', 'zh', 'x'), pairs)  13.3 us
  transfers between devices with their start and end apart: 138, of which 36 were waited for; matrix products, arithmetic and copies ran while one was open for 38% of the time, Pallas kernels for 0%

profile of v1, /device:TPU:1, one launch (start us, length us, event | category | flops | bytes accessed | tf_op | source)
XLA Modules:
  0.0 626.5 jit_solution(13260153389004333187)
XLA Ops:
  8.2 6.9 %collective-permute-start.20 = (bf16[2,64,1024]{2,1,0:T(8,128)(2,1)S(1)}, bf16[2,64,1024]{2,1,0:T(8,128)(2,1)S(1)}, u32[]{:S(2)}, u32[]{:S(2)}) collective-permute-start(bf16[2,64,1024]{2,1,0:T(8,128)(2,1)S(1)} %pad_maximum_fusion.9), channel_id=1, source_target_pairs={{0,0},{1,1},{2,2},{3,3},{4,8},{5,9},{6,10},{7,11},{8,4},{9,5},{10,... | collective-permute-start | bytes 786440 | tf_op jit(solution)/shard_map/ppermute | solution.py:42
  15.1 4.0 collective-permute-done.20
  21.4 5.1 collective-permute-start.5
  29.3 5.1 collective-permute-start
  45.4 4.7 all-to-all-start
  53.3 3.3 collective-permute-start.6
  60.5 9.2 %collective-permute-start.8 = (bf16[128,1024]{1,0:T(8,128)(2,1)S(1)}, bf16[128,1024]{1,0:T(8,128)(2,1)S(1)}, u32[]{:S(2)}, u32[]{:S(2)}) collective-permute-start(bf16[128,1024]{1,0:T(8,128)(2,1)S(1)} %collective-permute-done.7), channel_id=1, source_target_pairs={{0,8},{8,0},{1,9},{9,1},{2,10},{10,2},{3,11},{11,3},{4,12},{12,4},... | collective-permute-start | bytes 786440 | tf_op jit(solution)/shard_map/ppermute | solution.py:32
  97.7 3.7 collective-permute-done.16
  101.4 4.1 collective-permute-done.12
  113.2 4.1 collective-permute-done.27
  118.5 5.5 collective-permute-done.23
  126.4 4.0 multiply_convert_fusion.4
  131.9 3.5 multiply_convert_fusion.6
  136.0 3.5 multiply_convert_fusion.5
  140.6 3.5 multiply_convert_fusion.7
  155.7 4.4 collective-permute-done.22
  172.5 8.9 %all-gather.9.cloned.1.call-done = bf16[1,1024,512]{2,1,0:T(8,128)(2,1)} async-done(((bf16[1,64,512]{2,1,0:T(8,128)(2,1)}), bf16[1,1024,512]{2,1,0:T(8,128)(2,1)}) %all-gather.9.cloned.1.call-update) | async-done | bytes 1048592 | tf_op jit(solution)/shard_map/all_gather | solution.py:161
  184.9 11.0 %collective-permute-start.34 = (bf16[128,1024]{1,0:T(8,128)(2,1)}, bf16[128,1024]{1,0:T(8,128)(2,1)S(1)}, u32[]{:S(2)}, u32[]{:S(2)}) collective-permute-start(bf16[128,1024]{1,0:T(8,128)(2,1)} %collective-permute-done.33), channel_id=1, source_target_pairs={{0,8},{8,0},{1,9},{9,1},{2,10},{10,2},{3,11},{11,3},{4,12},{12,4},... | collective-permute-start | bytes 786440 | tf_op jit(solution)/shard_map/ppermute | solution.py:32
  217.5 2.9 collective-permute-start.43
  227.5 4.1 collective-permute-done.43
  231.6 3.4 collective-permute-done.45
  248.5 12.9 %all-gather.11.cloned.1.call-done = bf16[1,1024,1024]{2,1,0:T(8,128)(2,1)} async-done(((bf16[1,64,1024]{2,1,0:T(8,128)(2,1)}), bf16[1,1024,1024]{2,1,0:T(8,128)(2,1)}) %all-gather.11.cloned.1.call-update) | async-done | bytes 2097168 | tf_op jit(solution)/shard_map/all_gather | solution.py:162
  261.4 3.0 multiply_convert_fusion
  265.0 10.4 %collective-permute-start.60 = (bf16[128,1024]{1,0:T(8,128)(2,1)S(1)}, bf16[128,1024]{1,0:T(8,128)(2,1)S(1)}, u32[]{:S(2)}, u32[]{:S(2)}) collective-permute-start(bf16[128,1024]{1,0:T(8,128)(2,1)S(1)} %slice.1676), channel_id=1, source_target_pairs={{0,8},{8,0},{1,9},{9,1},{2,10},{10,2},{3,11},{11,3},{4,12},{12,4},... | collective-permute-start | bytes 786440 | tf_op jit(solution)/shard_map/ppermute | solution.py:32
  295.8 6.6 %collective-permute-done.54 = bf16[128,1024]{1,0:T(8,128)(2,1)S(1)} collective-permute-done((bf16[128,1024]{1,0:T(8,128)(2,1)S(1)}, bf16[128,1024]{1,0:T(8,128)(2,1)S(1)}, u32[]{:S(2)}, u32[]{:S(2)}) %collective-permute-start.54) | collective-permute-done | bytes 262176 | tf_op jit(solution)/shard_map/ppermute | solution.py:28
  302.4 3.0 collective-permute-done.50
  313.1 10.9 %collective-permute-done.67 = bf16[128,1024]{1,0:T(8,128)(2,1)S(1)} collective-permute-done((bf16[128,1024]{1,0:T(8,128)(2,1)S(1)}, bf16[128,1024]{1,0:T(8,128)(2,1)S(1)}, u32[]{:S(2)}, u32[]{:S(2)}) %collective-permute-start.67) | collective-permute-done | bytes 262176 | tf_op jit(solution)/shard_map/ppermute | solution.py:28
  343.8 3.9 copy.71
  347.9 5.4 collective-permute-done.74
  353.3 3.6 multiply_reduce_fusion
  403.1 5.5 collective-permute-done.89
  408.6 4.0 collective-permute-done.85
  429.7 5.9 collective-permute-start.100
  445.0 3.9 convolution_convert_fusion.3
  450.7 3.4 collective-permute-start.98
  459.8 3.5 collective-permute-done.102
  463.3 4.4 collective-permute-done.94
  478.1 2.8 collective-permute-start.110
  486.3 3.9 collective-permute-start.111
  519.7 5.4 all-to-all-start.1
  534.1 6.2 collective-permute-start.61
  540.3 3.8 collective-permute-done.113
  544.4 6.1 collective-permute-start.119
  550.4 4.9 collective-permute-done.61
  556.1 3.8 collective-permute-done.119
  563.6 3.3 collective-permute-start.127
  571.2 23.4 %reduce-scatter.12.cloned.1.call-done = bf16[64,1024]{1,0:T(8,128)(2,1)} async-done(((bf16[1024,1024]{1,0:T(8,128)(2,1)}), bf16[64,1024]{1,0:T(8,128)(2,1)}) %reduce-scatter.12.cloned.1.call-update) | async-done | bytes 131088
  596.1 14.8 %collective-permute-start.124 = (bf16[2,64,1536]{2,1,0:T(8,128)(2,1)S(1)}, bf16[2,64,1536]{2,1,0:T(8,128)(2,1)S(1)}, u32[]{:S(2)}, u32[]{:S(2)}) collective-permute-start(bf16[2,64,1536]{2,1,0:T(8,128)(2,1)S(1)} %copy.62), channel_id=1, source_target_pairs={{0,0},{1,1},{2,2},{3,3},{4,8},{5,9},{6,10},{7,11},{8,4},{9,5},{10,... | collective-permute-start | bytes 1179656 | tf_op jit(solution)/shard_map/ppermute | solution.py:42
  (1056 shorter events, 334.3 us)
Async XLA Ops:
  7.2 119.2 %all-gather.7.cloned.1.call-start = ((), (), s32[]{:S(2)}) async-start(), calls=%async_computation.5 | async-start | bytes 2228224 | tf_op jit(solution)/shard_map/all_gather | solution.py:159
  19.9 161.5 %all-gather.9.cloned.1.call-start = ((), (), s32[]{:S(2)}) async-start(), calls=%async_computation.6 | async-start | bytes 1114112 | tf_op jit(solution)/shard_map/all_gather | solution.py:161
  20.7 23.5 %collective-permute-start.1 = (f32[1024]{0:T(1024)S(1)}, f32[1024]{0:T(1024)S(1)}, u32[]{:S(2)}, u32[]{:S(2)}) collective-permute-start(f32[1024]{0:T(1024)S(1)} %add_convert_fusion.9), channel_id=1, source_target_pairs={{0,8},{8,0},{1,9},{9,1},{2,10},{10,2},{3,11},{11,3},{4,12},{12,4},... | collective-permute-start | bytes 12296 | tf_op jit(solution)/shard_map/ppermute | solution.py:32
  21.4 28.8 %collective-permute-start.5 = (f32[2,768]{1,0:T(2,128)S(1)}, f32[2,768]{1,0:T(2,128)S(1)}, u32[]{:S(2)}, u32[]{:S(2)}) collective-permute-start(f32[2,768]{1,0:T(2,128)S(1)} %pad_maximum_fusion.15), channel_id=1, source_target_pairs={{0,0},{1,1},{2,2},{3,3},{4,8},{5,9},{6,10},{7,11},{8,4},{9,5},{10,... | collective-permute-start | bytes 18440 | tf_op jit(solution)/shard_map/ppermute | solution.py:42
  29.3 21.5 %collective-permute-start = (bf16[128,1024]{1,0:T(8,128)(2,1)}, bf16[128,1024]{1,0:T(8,128)(2,1)S(1)}, u32[]{:S(2)}, u32[]{:S(2)}) collective-permute-start(bf16[128,1024]{1,0:T(8,128)(2,1)} %param.19), channel_id=1, source_target_pairs={{0,0},{1,1},{2,2},{3,3},{4,8},{5,9},{6,10},{7,11},{8,4},{9,5},{10,... | collective-permute-start | bytes 786440 | tf_op jit(solution)/shard_map/ppermute | solution.py:42
  34.5 271.6 %collective-permute-start.62 = (bf16[128,1024]{1,0:T(8,128)(2,1)}, bf16[128,1024]{1,0:T(8,128)(2,1)S(1)}, u32[]{:S(2)}, u32[]{:S(2)}) collective-permute-start(bf16[128,1024]{1,0:T(8,128)(2,1)} %param.20), channel_id=1, source_target_pairs={{0,0},{1,1},{2,2},{3,3},{4,8},{5,9},{6,10},{7,11},{8,4},{9,5},{10,... | collective-permute-start | bytes 786440 | tf_op jit(solution)/shard_map/ppermute | solution.py:42
  45.4 26.1 %all-to-all-start = ((bf16[16,64,512]{2,1,0:T(8,128)(2,1)}), bf16[16,64,512]{2,1,0:T(8,128)(2,1)S(1)}, u32[]{:S(2)}, u32[]{:S(2)}) async-start(bf16[16,64,512]{2,1,0:T(8,128)(2,1)} %broadcast_in_dim.36), calls=%async_computation | async-start | bytes 2097152 | tf_op jit(solution)/shard_map/all_to_all | solution.py:158
  50.1 211.3 %all-gather.11.cloned.1.call-start = ((), (), s32[]{:S(2)}) async-start(), calls=%async_computation.7 | async-start | bytes 2228224 | tf_op jit(solution)/shard_map/all_gather | solution.py:162
  53.3 16.5 %collective-permute-start.6 = (bf16[128,1024]{1,0:T(8,128)(2,1)S(1)}, bf16[128,1024]{1,0:T(8,128)(2,1)}, u32[]{:S(2)}, u32[]{:S(2)}) collective-permute-start(bf16[128,1024]{1,0:T(8,128)(2,1)S(1)} %collective-permute-done), channel_id=1, source_target_pairs={{0,8},{8,0},{1,9},{9,1},{2,10},{10,2},{3,11},{11,3},{4,12},{12,4},... | collective-permute-start | bytes 786440 | tf_op jit(solution)/shard_map/ppermute | solution.py:32
  59.3 501.5 %reduce-scatter.14.cloned.1.call-start = ((), (), s32[]{:S(2)}) async-start(), calls=%async_computation.10 | async-start | bytes 2228224
  106.9 18.0 %collective-permute-start.31 = (bf16[128,1024]{1,0:T(8,128)(2,1)S(1)}, bf16[128,1024]{1,0:T(8,128)(2,1)S(1)}, u32[]{:S(2)}, u32[]{:S(2)}) collective-permute-start(bf16[128,1024]{1,0:T(8,128)(2,1)S(1)} %get-tuple-element.85), channel_id=1, source_target_pairs={{0,8},{8,0},{1,9},{9,1},{2,10},{10,2},{3,11},{11,3},{4,12},{12,4},... | collective-permute-start | bytes 786440 | tf_op jit(solution)/shard_map/ppermute | solution.py:32
  109.3 14.7 %collective-permute-start.23 = (bf16[128,1024]{1,0:T(8,128)(2,1)S(1)}, bf16[128,1024]{1,0:T(8,128)(2,1)}, u32[]{:S(2)}, u32[]{:S(2)}) collective-permute-start(bf16[128,1024]{1,0:T(8,128)(2,1)S(1)} %get-tuple-element.85), channel_id=1, source_target_pairs={{0,1},{1,2},{2,3},{3,0},{4,5},{5,6},{6,7},{7,4},{8,9},{9,10},{10,1... | collective-permute-start | bytes 786440 | tf_op jit(solution)/shard_map/ppermute | solution.py:28
  110.7 14.2 %collective-permute-start.18 = (bf16[128,1024]{1,0:T(8,128)(2,1)S(1)}, bf16[128,1024]{1,0:T(8,128)(2,1)}, u32[]{:S(2)}, u32[]{:S(2)}) collective-permute-start(bf16[128,1024]{1,0:T(8,128)(2,1)S(1)} %get-tuple-element.85), channel_id=1, source_target_pairs={{0,2},{1,3},{2,0},{3,1},{4,6},{5,7},{6,4},{7,5},{8,10},{9,11},{10,... | collective-permute-start | bytes 786440 | tf_op jit(solution)/shard_map/ppermute | solution.py:28
  117.3 18.7 %collective-permute-start.28 = (bf16[128,1024]{1,0:T(8,128)(2,1)}, bf16[128,1024]{1,0:T(8,128)(2,1)}, u32[]{:S(2)}, u32[]{:S(2)}) collective-permute-start(bf16[128,1024]{1,0:T(8,128)(2,1)} %collective-permute-done.27), channel_id=1, source_target_pairs={{0,8},{8,0},{1,9},{9,1},{2,10},{10,2},{3,11},{11,3},{4,12},{12,4},... | collective-permute-start | bytes 786440 | tf_op jit(solution)/shard_map/ppermute | solution.py:32
  124.9 15.6 %collective-permute-start.19 = (bf16[128,1024]{1,0:T(8,128)(2,1)}, bf16[128,1024]{1,0:T(8,128)(2,1)}, u32[]{:S(2)}, u32[]{:S(2)}) collective-permute-start(bf16[128,1024]{1,0:T(8,128)(2,1)} %collective-permute-done.18), channel_id=1, source_target_pairs={{0,8},{8,0},{1,9},{9,1},{2,10},{10,2},{3,11},{11,3},{4,12},{12,4},... | collective-permute-start | bytes 786440 | tf_op jit(solution)/shard_map/ppermute | solution.py:32
  130.9 22.5 %collective-permute-start.32 = (bf16[128,1024]{1,0:T(8,128)(2,1)S(1)}, bf16[128,1024]{1,0:T(8,128)(2,1)S(1)}, u32[]{:S(2)}, u32[]{:S(2)}) collective-permute-start(bf16[128,1024]{1,0:T(8,128)(2,1)S(1)} %slice.1684), channel_id=1, source_target_pairs={{0,8},{8,0},{1,9},{9,1},{2,10},{10,2},{3,11},{11,3},{4,12},{12,4},... | collective-permute-start | bytes 786440 | tf_op jit(solution)/shard_map/ppermute | solution.py:32
  163.6 17.8 %collective-permute-start.35 = (bf16[128,1024]{1,0:T(8,128)(2,1)S(1)}, bf16[128,1024]{1,0:T(8,128)(2,1)}, u32[]{:S(2)}, u32[]{:S(2)}) collective-permute-start(bf16[128,1024]{1,0:T(8,128)(2,1)S(1)} %get-tuple-element.83), channel_id=1, source_target_pairs={{0,8},{8,0},{1,9},{9,1},{2,10},{10,2},{3,11},{11,3},{4,12},{12,4},... | collective-permute-start | bytes 786440 | tf_op jit(solution)/shard_map/ppermute | solution.py:32
  170.9 14.0 %collective-permute-start.33 = (bf16[128,1024]{1,0:T(8,128)(2,1)S(1)}, bf16[128,1024]{1,0:T(8,128)(2,1)}, u32[]{:S(2)}, u32[]{:S(2)}) collective-permute-start(bf16[128,1024]{1,0:T(8,128)(2,1)S(1)} %get-tuple-element.83), channel_id=1, source_target_pairs={{0,2},{1,3},{2,0},{3,1},{4,6},{5,7},{6,4},{7,5},{8,10},{9,11},{10,... | collective-permute-start | bytes 786440 | tf_op jit(solution)/shard_map/ppermute | solution.py:28
  171.4 24.5 %collective-permute-start.39 = (bf16[128,1024]{1,0:T(8,128)(2,1)}, bf16[128,1024]{1,0:T(8,128)(2,1)}, u32[]{:S(2)}, u32[]{:S(2)}) collective-permute-start(bf16[128,1024]{1,0:T(8,128)(2,1)} %collective-permute-done.38), channel_id=1, source_target_pairs={{0,8},{8,0},{1,9},{9,1},{2,10},{10,2},{3,11},{11,3},{4,12},{12,4},... | collective-permute-start | bytes 786440 | tf_op jit(solution)/shard_map/ppermute | solution.py:32
  171.7 25.7 %collective-permute-start.37 = (bf16[128,1024]{1,0:T(8,128)(2,1)}, bf16[128,1024]{1,0:T(8,128)(2,1)}, u32[]{:S(2)}, u32[]{:S(2)}) collective-permute-start(bf16[128,1024]{1,0:T(8,128)(2,1)} %collective-permute-done.36), channel_id=1, source_target_pairs={{0,8},{8,0},{1,9},{9,1},{2,10},{10,2},{3,11},{11,3},{4,12},{12,4},... | collective-permute-start | bytes 786440 | tf_op jit(solution)/shard_map/ppermute | solution.py:32
  184.9 14.1 %collective-permute-start.34 = (bf16[128,1024]{1,0:T(8,128)(2,1)}, bf16[128,1024]{1,0:T(8,128)(2,1)S(1)}, u32[]{:S(2)}, u32[]{:S(2)}) collective-permute-start(bf16[128,1024]{1,0:T(8,128)(2,1)} %collective-permute-done.33), channel_id=1, source_target_pairs={{0,8},{8,0},{1,9},{9,1},{2,10},{10,2},{3,11},{11,3},{4,12},{12,4},... | collective-permute-start | bytes 786440 | tf_op jit(solution)/shard_map/ppermute | solution.py:32
  213.0 14.5 %collective-permute-start.46 = (bf16[128,1024]{1,0:T(8,128)(2,1)S(1)}, bf16[128,1024]{1,0:T(8,128)(2,1)S(1)}, u32[]{:S(2)}, u32[]{:S(2)}) collective-permute-start(bf16[128,1024]{1,0:T(8,128)(2,1)S(1)} %slice.1680), channel_id=1, source_target_pairs={{0,8},{8,0},{1,9},{9,1},{2,10},{10,2},{3,11},{11,3},{4,12},{12,4},... | collective-permute-start | bytes 786440 | tf_op jit(solution)/shard_map/ppermute | solution.py:32
  217.5 14.1 %collective-permute-start.43 = (bf16[128,1024]{1,0:T(8,128)(2,1)S(1)}, bf16[128,1024]{1,0:T(8,128)(2,1)S(1)}, u32[]{:S(2)}, u32[]{:S(2)}) collective-permute-start(bf16[128,1024]{1,0:T(8,128)(2,1)S(1)} %fusion.146), channel_id=1, source_target_pairs={{0,3},{1,0},{2,1},{3,2},{4,7},{5,4},{6,5},{7,6},{8,11},{9,8},{10,9... | collective-permute-start | bytes 786440 | tf_op jit(solution)/shard_map/ppermute | solution.py:28
  220.5 14.5 %collective-permute-start.45 = (bf16[128,1024]{1,0:T(8,128)(2,1)S(1)}, bf16[128,1024]{1,0:T(8,128)(2,1)S(1)}, u32[]{:S(2)}, u32[]{:S(2)}) collective-permute-start(bf16[128,1024]{1,0:T(8,128)(2,1)S(1)} %fusion.145), channel_id=1, source_target_pairs={{0,1},{1,2},{2,3},{3,0},{4,5},{5,6},{6,7},{7,4},{8,9},{9,10},{10,1... | collective-permute-start | bytes 786440 | tf_op jit(solution)/shard_map/ppermute | solution.py:28
  220.7 14.3 %collective-permute-start.41 = (bf16[128,1024]{1,0:T(8,128)(2,1)S(1)}, bf16[128,1024]{1,0:T(8,128)(2,1)S(1)}, u32[]{:S(2)}, u32[]{:S(2)}) collective-permute-start(bf16[128,1024]{1,0:T(8,128)(2,1)S(1)} %fusion.147), channel_id=1, source_target_pairs={{0,2},{1,3},{2,0},{3,1},{4,6},{5,7},{6,4},{7,5},{8,10},{9,11},{10,... | collective-permute-start | bytes 786440 | tf_op jit(solution)/shard_map/ppermute | solution.py:28
  237.2 24.3 %collective-permute-start.59 = (bf16[128,1024]{1,0:T(8,128)(2,1)}, bf16[128,1024]{1,0:T(8,128)(2,1)}, u32[]{:S(2)}, u32[]{:S(2)}) collective-permute-start(bf16[128,1024]{1,0:T(8,128)(2,1)} %get-tuple-element.87), channel_id=1, source_target_pairs={{0,8},{8,0},{1,9},{9,1},{2,10},{10,2},{3,11},{11,3},{4,12},{12,4},... | collective-permute-start | bytes 786440 | tf_op jit(solution)/shard_map/ppermute | solution.py:32
  242.4 33.1 %collective-permute-start.55 = (bf16[128,1024]{1,0:T(8,128)(2,1)}, bf16[128,1024]{1,0:T(8,128)(2,1)}, u32[]{:S(2)}, u32[]{:S(2)}) collective-permute-start(bf16[128,1024]{1,0:T(8,128)(2,1)} %get-tuple-element.87), channel_id=1, source_target_pairs={{0,3},{1,0},{2,1},{3,2},{4,7},{5,4},{6,5},{7,6},{8,11},{9,8},{10,9... | collective-permute-start | bytes 786440 | tf_op jit(solution)/shard_map/ppermute | solution.py:28
  245.0 30.5 %collective-permute-start.47 = (bf16[128,1024]{1,0:T(8,128)(2,1)}, bf16[128,1024]{1,0:T(8,128)(2,1)}, u32[]{:S(2)}, u32[]{:S(2)}) collective-permute-start(bf16[128,1024]{1,0:T(8,128)(2,1)} %get-tuple-element.87), channel_id=1, source_target_pairs={{0,2},{1,3},{2,0},{3,1},{4,6},{5,7},{6,4},{7,5},{8,10},{9,11},{10,... | collective-permute-start | bytes 786440 | tf_op jit(solution)/shard_map/ppermute | solution.py:28
  247.8 30.2 %collective-permute-start.52 = (bf16[128,1024]{1,0:T(8,128)(2,1)}, bf16[128,1024]{1,0:T(8,128)(2,1)}, u32[]{:S(2)}, u32[]{:S(2)}) collective-permute-start(bf16[128,1024]{1,0:T(8,128)(2,1)} %collective-permute-done.51), channel_id=1, source_target_pairs={{0,8},{8,0},{1,9},{9,1},{2,10},{10,2},{3,11},{11,3},{4,12},{12,4},... | collective-permute-start | bytes 786440 | tf_op jit(solution)/shard_map/ppermute | solution.py:32
  265.0 30.8 %collective-permute-start.60 = (bf16[128,1024]{1,0:T(8,128)(2,1)S(1)}, bf16[128,1024]{1,0:T(8,128)(2,1)S(1)}, u32[]{:S(2)}, u32[]{:S(2)}) collective-permute-start(bf16[128,1024]{1,0:T(8,128)(2,1)S(1)} %slice.1676), channel_id=1, source_target_pairs={{0,8},{8,0},{1,9},{9,1},{2,10},{10,2},{3,11},{11,3},{4,12},{12,4},... | collective-permute-start | bytes 786440 | tf_op jit(solution)/shard_map/ppermute | solution.py:32
  291.5 13.9 %collective-permute-start.50 = (bf16[128,1024]{1,0:T(8,128)(2,1)S(1)}, bf16[128,1024]{1,0:T(8,128)(2,1)S(1)}, u32[]{:S(2)}, u32[]{:S(2)}) collective-permute-start(bf16[128,1024]{1,0:T(8,128)(2,1)S(1)} %fusion.141), channel_id=1, source_target_pairs={{0,2},{1,3},{2,0},{3,1},{4,6},{5,7},{6,4},{7,5},{8,10},{9,11},{10,... | collective-permute-start | bytes 786440 | tf_op jit(solution)/shard_map/ppermute | solution.py:28
  307.7 17.2 %collective-permute-start.75 = (bf16[128,1024]{1,0:T(8,128)(2,1)S(1)}, bf16[128,1024]{1,0:T(8,128)(2,1)S(1)}, u32[]{:S(2)}, u32[]{:S(2)}) collective-permute-start(bf16[128,1024]{1,0:T(8,128)(2,1)S(1)} %get-tuple-element.78), channel_id=1, source_target_pairs={{0,8},{8,0},{1,9},{9,1},{2,10},{10,2},{3,11},{11,3},{4,12},{12,4},... | collective-permute-start | bytes 786440 | tf_op jit(solution)/shard_map/ppermute | solution.py:32
  309.3 14.7 %collective-permute-start.67 = (bf16[128,1024]{1,0:T(8,128)(2,1)S(1)}, bf16[128,1024]{1,0:T(8,128)(2,1)S(1)}, u32[]{:S(2)}, u32[]{:S(2)}) collective-permute-start(bf16[128,1024]{1,0:T(8,128)(2,1)S(1)} %get-tuple-element.78), channel_id=1, source_target_pairs={{0,1},{1,2},{2,3},{3,0},{4,5},{5,6},{6,7},{7,4},{8,9},{9,10},{10,1... | collective-permute-start | bytes 786440 | tf_op jit(solution)/shard_map/ppermute | solution.py:28
  310.3 18.0 %collective-permute-start.71 = (bf16[128,1024]{1,0:T(8,128)(2,1)S(1)}, bf16[128,1024]{1,0:T(8,128)(2,1)S(1)}, u32[]{:S(2)}, u32[]{:S(2)}) collective-permute-start(bf16[128,1024]{1,0:T(8,128)(2,1)S(1)} %get-tuple-element.78), channel_id=1, source_target_pairs={{0,3},{1,0},{2,1},{3,2},{4,7},{5,4},{6,5},{7,6},{8,11},{9,8},{10,9... | collective-permute-start | bytes 786440 | tf_op jit(solution)/shard_map/ppermute | solution.py:28
  313.0 15.7 %collective-permute-start.63 = (bf16[128,1024]{1,0:T(8,128)(2,1)S(1)}, bf16[128,1024]{1,0:T(8,128)(2,1)S(1)}, u32[]{:S(2)}, u32[]{:S(2)}) collective-permute-start(bf16[128,1024]{1,0:T(8,128)(2,1)S(1)} %get-tuple-element.78), channel_id=1, source_target_pairs={{0,2},{1,3},{2,0},{3,1},{4,6},{5,7},{6,4},{7,5},{8,10},{9,11},{10,... | collective-permute-start | bytes 786440 | tf_op jit(solution)/shard_map/ppermute | solution.py:28
  328.3 19.6 %collective-permute-start.76 = (bf16[128,1024]{1,0:T(8,128)(2,1)}, bf16[128,1024]{1,0:T(8,128)(2,1)}, u32[]{:S(2)}, u32[]{:S(2)}) collective-permute-start(bf16[128,1024]{1,0:T(8,128)(2,1)} %slice.1672), channel_id=1, source_target_pairs={{0,8},{8,0},{1,9},{9,1},{2,10},{10,2},{3,11},{11,3},{4,12},{12,4},... | collective-permute-start | bytes 786440 | tf_op jit(solution)/shard_map/ppermute | solution.py:32
  338.7 14.6 %collective-permute-start.74 = (bf16[128,1024]{1,0:T(8,128)(2,1)}, bf16[128,1024]{1,0:T(8,128)(2,1)}, u32[]{:S(2)}, u32[]{:S(2)}) collective-permute-start(bf16[128,1024]{1,0:T(8,128)(2,1)} %fusion.133), channel_id=1, source_target_pairs={{0,1},{1,2},{2,3},{3,0},{4,5},{5,6},{6,7},{7,4},{8,9},{9,10},{10,1... | collective-permute-start | bytes 786440 | tf_op jit(solution)/shard_map/ppermute | solution.py:28
  347.8 221.0 %reduce-scatter.10.cloned.1.call-start = ((), (), s32[]{:S(2)}) async-start(), calls=%async_computation.8 | async-start | bytes 1114112 | tf_op jit(solution)/shard_map/reduce_scatter | solution.py:290
  420.9 173.7 %reduce-scatter.12.cloned.1.call-start = ((), (), s32[]{:S(2)}) async-start(), calls=%async_computation.9 | async-start | bytes 2228224
  429.6 28.8 %collective-permute-start.104 = (bf16[128,1024]{1,0:T(8,128)(2,1)S(1)}, bf16[128,1024]{1,0:T(8,128)(2,1)S(1)}, u32[]{:S(2)}, u32[]{:S(2)}) collective-permute-start(bf16[128,1024]{1,0:T(8,128)(2,1)S(1)} %slice.1664), channel_id=1, source_target_pairs={{0,8},{8,0},{1,9},{9,1},{2,10},{10,2},{3,11},{11,3},{4,12},{12,4},... | collective-permute-start | bytes 786440 | tf_op jit(solution)/shard_map/ppermute | solution.py:32
  508.3 19.3 %collective-permute-start.116 = (bf16[128,1024]{1,0:T(8,128)(2,1)S(1)}, bf16[128,1024]{1,0:T(8,128)(2,1)}, u32[]{:S(2)}, u32[]{:S(2)}) collective-permute-start(bf16[128,1024]{1,0:T(8,128)(2,1)S(1)} %slice.1661), channel_id=1, source_target_pairs={{0,8},{8,0},{1,9},{9,1},{2,10},{10,2},{3,11},{11,3},{4,12},{12,4},... | collective-permute-start | bytes 786440 | tf_op jit(solution)/shard_map/ppermute | solution.py:32
  519.7 42.2 %all-to-all-start.1 = ((bf16[16,80,512]{2,1,0:T(8,128)(2,1)}), bf16[16,80,512]{2,1,0:T(8,128)(2,1)S(1)}, u32[]{:S(2)}, u32[]{:S(2)}) async-start(bf16[16,80,512]{2,1,0:T(8,128)(2,1)} %pad_maximum_fusion.2), calls=%async_computation.1 | async-start | bytes 2621440 | tf_op jit(solution)/shard_map/all_to_all | solution.py:315
  525.2 15.0 %collective-permute-start.118 = (bf16[128,1024]{1,0:T(8,128)(2,1)S(1)}, bf16[128,1024]{1,0:T(8,128)(2,1)S(1)}, u32[]{:S(2)}, u32[]{:S(2)}) collective-permute-start(bf16[128,1024]{1,0:T(8,128)(2,1)S(1)} %slice.1660), channel_id=1, source_target_pairs={{0,8},{8,0},{1,9},{9,1},{2,10},{10,2},{3,11},{11,3},{4,12},{12,4},... | collective-permute-start | bytes 786440 | tf_op jit(solution)/shard_map/ppermute | solution.py:32
  534.1 21.2 %collective-permute-start.61 = (bf16[128,1024]{1,0:T(8,128)(2,1)S(1)}, bf16[128,1024]{1,0:T(8,128)(2,1)S(1)}, u32[]{:S(2)}, u32[]{:S(2)}) collective-permute-start(bf16[128,1024]{1,0:T(8,128)(2,1)S(1)} %copy-done.67), channel_id=1, source_target_pairs={{0,0},{1,1},{2,2},{3,3},{4,8},{5,9},{6,10},{7,11},{8,4},{9,5},{10,... | collective-permute-start | bytes 786440 | tf_op jit(solution)/shard_map/ppermute | solution.py:42
  544.4 15.6 %collective-permute-start.119 = (bf16[128,1024]{1,0:T(8,128)(2,1)S(1)}, bf16[128,1024]{1,0:T(8,128)(2,1)S(1)}, u32[]{:S(2)}, u32[]{:S(2)}) collective-permute-start(bf16[128,1024]{1,0:T(8,128)(2,1)S(1)} %fusion.117), channel_id=1, source_target_pairs={{0,0},{1,1},{2,2},{3,3},{4,8},{5,9},{6,10},{7,11},{8,4},{9,5},{10,... | collective-permute-start | bytes 786440 | tf_op jit(solution)/shard_map/ppermute | solution.py:42
  566.9 44.0 %collective-permute-start.125 = (f32[2,768]{1,0:T(2,128)S(1)}, f32[2,768]{1,0:T(2,128)S(1)}, u32[]{:S(2)}, u32[]{:S(2)}) collective-permute-start(f32[2,768]{1,0:T(2,128)S(1)} %reshape.250), channel_id=1, source_target_pairs={{0,0},{1,1},{2,2},{3,3},{4,8},{5,9},{6,10},{7,11},{8,4},{9,5},{10,... | collective-permute-start | bytes 18440 | tf_op jit(solution)/shard_map/ppermute | solution.py:42
  571.1 40.9 %collective-permute-start.129 = (f32[1,4,12,128]{3,1,0,2:T(4,128)S(1)}, f32[1,4,12,128]{3,1,0,2:T(4,128)S(1)}, u32[]{:S(2)}, u32[]{:S(2)}) collective-permute-start(f32[1,4,12,128]{3,1,0,2:T(4,128)S(1)} %constant_dynamic-slice_fusion), channel_id=1, source_target_pairs={{0,8},{8,0},{1,9},{9,1},{2,10},{10,2},{3,11},{11,3},{4,12},{12,4},... | collective-permute-start | bytes 73736 | tf_op jit(solution)/shard_map/ppermute | solution.py:32
  596.1 20.2 %collective-permute-start.124 = (bf16[2,64,1536]{2,1,0:T(8,128)(2,1)S(1)}, bf16[2,64,1536]{2,1,0:T(8,128)(2,1)S(1)}, u32[]{:S(2)}, u32[]{:S(2)}) collective-permute-start(bf16[2,64,1536]{2,1,0:T(8,128)(2,1)S(1)} %copy.62), channel_id=1, source_target_pairs={{0,0},{1,1},{2,2},{3,3},{4,8},{5,9},{6,10},{7,11},{8,4},{9,5},{10,... | collective-permute-start | bytes 1179656 | tf_op jit(solution)/shard_map/ppermute | solution.py:42
  (268 other events, 1900.2 us)
Sparse Core Ops, SparseCore 0:
  20.0 85.3 all-gather.6
  107.6 73.7 all-gather.8
  183.0 78.3 all-gather.10
  347.9 72.0 reduce-scatter.13
  422.2 75.6 reduce-scatter.9
  500.2 94.3 reduce-scatter.11
